TPU v7x, 128 devices: a whole 4x4x4 slice. The times are simulated.
128 devices in a mesh: row: 8 (over y_lo, z), col: 16 (over x, y_hi, core).
Axes of the slice: x: 4, y: 4 (y_hi: 2, y_lo: 2; y = y_hi * 2 + y_lo), z: 4, core: 2. Of those that a mesh axis runs over, the one named last changes fastest.
Arguments:
- amplitudes: float32 [512, 20480], P('row', 'col'), may hold values from -6 to 6
- integrals: float32 [512, 38400], P('col', 'row'), may hold values from -0.25 to 0.25
Outputs:
- residual: float32 [38400, 20480], P('row', 'col')
All inputs are finite; a program needn't handle non-finite values.
Results may differ from a plain program's by a relative error of at most 0.00007.
Values sent between devices are 32-bit elements; how exact they have to be, the bound alone decides.
No kernel may reach another device: no remote copies, remote signals or barrier semaphores. Data moves between devices by JAX's collectives and lax.ppermute only.
A program may use at most 128 MiB of HBM per device.

v0:
```python
import jax
import jax.numpy as jnp
from jax import lax
from jax.sharding import PartitionSpec as P


def contract_rows(left_block, right_block):
    return lax.dot_general(
        left_block,
        right_block,
        (((0,), (0,)), ((), ())),
        precision=lax.Precision.HIGHEST,
        preferred_element_type=jnp.float32,
    )


def ladder(amps_block, integral_block):
    whole_amps = lax.all_gather(amps_block, "row", axis=0, tiled=True)
    return contract_rows(lax.all_gather(integral_block, "col", axis=0, tiled=True), whole_amps)


def body(amplitudes, integrals):
    return 0.5 * ladder(amplitudes, integrals)


def solution(mesh):
    in_specs = (P("row", "col"), P("col", "row"))
    out_specs = P("row", "col")
    return jax.shard_map(body, mesh=mesh, in_specs=in_specs, out_specs=out_specs, check_vma=False)
```

profile of v0, /device:TPU:1, one launch (start us, length us, event | category | flops | bytes accessed | tf_op | source)
XLA Modules:
  0.0 227.3 jit_solution(12496698475896982546)
XLA Ops:
  6.5 0.0 all-gather.5.cloned.1.call-start
  6.5 0.7 all-gather.5.cloned.1.call-update
  7.3 0.0 all-gather.3.cloned.1.call-start
  7.3 0.7 all-gather.3.cloned.1.call-update
  8.0 42.6 %all-gather.5.cloned.1.call-done = f32[512,1280]{1,0:T(8,128)} async-done(((f32[64,1280]{1,0:T(8,128)}), f32[512,1280]{1,0:T(8,128)}) %all-gather.5.cloned.1.call-update) | async-done | bytes 2621456 | tf_op jit(solution)/shard_map/all_gather | solution.py:18
  50.6 85.5 %all-gather.3.cloned.1.call-done = f32[512,4800]{1,0:T(8,128)} async-done(((f32[32,4800]{1,0:T(8,128)}), f32[512,4800]{1,0:T(8,128)}) %all-gather.3.cloned.1.call-update) | async-done | bytes 9830416 | tf_op jit(solution)/shard_map/all_gather | solution.py:19
  136.0 84.5 %convolution_multiply_fusion = f32[4800,1280]{1,0:T(8,128)} fusion(f32[512,4800]{1,0:T(8,128)} %all-gather.3.cloned.1.call-done, f32[512,1280]{1,0:T(8,128)} %all-gather.5.cloned.1.call-done), kind=kOutput, calls=%fused_computation | convolution fusion | flops 37754880000 | bytes 37027840 | tf_op jit(solution)/shard_map/dot_general | solution.py:8
Async XLA Ops:
  6.5 44.0 %all-gather.5.cloned.1.call-start = ((), (), s32[]{:S(2)}) async-start(), calls=%async_computation.1 | async-start | bytes 2949120 | tf_op jit(solution)/shard_map/all_gather | solution.py:18
  7.3 128.8 %all-gather.3.cloned.1.call-start = ((), (), s32[]{:S(2)}) async-start(), calls=%async_computation | async-start | bytes 10584064 | tf_op jit(solution)/shard_map/all_gather | solution.py:19
Sparse Core Ops, SparseCore 0:
  9.0 41.5 all-gather.4
  53.0 83.0 all-gather.2
where the time goes:
time: 227 us
  waiting for transfers between devices  129 us (57%)
  matrix products  84.5 us (37%)
  between operations  13.4 us (6%)
    all_gather x1, waiting for transfers between devices, ladder(): lax.all_gather(integral_block, 'col', axis=0, tiled=True)  85.5 us
    dot_general x1, matrix products, contract_rows(): lax.dot_general(left_block, right_block, (((0,), (0,)), ((), ())), precis...  84.5 us
    all_gather x1, waiting for transfers between devices, ladder(): whole_amps = lax.all_gather(amps_block, 'row', axis=0, tiled=True)  42.6 us
  transfers between devices with their start and end apart: 2, of which 2 were waited for; matrix products, arithmetic and copies ran while one was open for 0% of the time, Pallas kernels for 0%

commit v1 on v0

v1 whole, which is shorter than its diff:
```python
import jax
import jax.numpy as jnp
from jax import lax
from jax.experimental import pallas as pl
from jax.experimental.pallas import tpu as pltpu
from jax.sharding import PartitionSpec as P

NZ, NX = 4, 4
BF, F32 = jnp.bfloat16, jnp.float32
WIDE = 1280
CHUNKS = ((1280, 1280, 320), (2560, 1280, 320), (3840, 960, 240))
EARLY = False
CUT_AT = 1


def swap_core(v):
    return lax.ppermute(v, "col", [(i, i ^ 1) for i in range(16)])


def swap_y_hi(v):
    return lax.ppermute(v, "col", [(i, i ^ 2) for i in range(16)])


def swap_y_lo(v):
    return lax.ppermute(v, "row", [(i, i ^ 4) for i in range(8)])


def shift_x(v):
    return lax.ppermute(v, "col", [(i, (i + (4 if i % 2 == 0 else 12)) % 16) for i in range(16)])


def send_x(v, d):
    return lax.ppermute(v, "col", [(i, (i + 4 * d) % 16) for i in range(16)])


def shift_z(v):
    pairs = []
    for row in range(8):
        for col in range(16):
            z = (row % 4 + (1 if col % 2 == 0 else 3)) % 4
            pairs.append((row * 16 + col, (row // 4 * 4 + z) * 16 + col))
    return lax.ppermute(v, ("row", "col"), pairs)


def tie(value, done):
    return lax.optimization_barrier((value, done))


def split(v):
    high = v.astype(BF)
    return high, (v - high.astype(F32)).astype(BF)


def amps_kernel(own, near, far, opposite, y_own, y_near, y_far, y_opposite, out):
    row, col = lax.axis_index("row"), lax.axis_index("col")
    y_lo, z = row // NZ, row % NZ
    x, step = col // 4, 1 - 2 * (col % 2)
    sides = ((y_lo, own, near, far, opposite), (1 - y_lo, y_own, y_near, y_far, y_opposite))
    for y, *pieces in sides:
        for piece, zz in zip(pieces, (z, z - step, z + step, z + 2)):
            high, low = split(piece[...] * 0.5)
            zz = (zz + NZ) % NZ
            slot = ((y * 2 + zz // 2 - x) * step + 2 * NX) % NX
            at = pl.multiple_of(slot * 128 + zz % 2 * 64, 64)
            out[pl.ds(at, 64), :] = high
            out[pl.ds(at + 512, 64), :] = high
            out[pl.ds(at + 1024, 64), :] = low


def stack_amps(pieces):
    pairs = pieces[0].shape[1]
    return pl.pallas_call(
        amps_kernel,
        grid=(pairs // 256,),
        out_shape=jax.ShapeDtypeStruct((1536, pairs), BF),
        in_specs=[pl.BlockSpec((64, 256), lambda i: (0, i))] * 8,
        out_specs=pl.BlockSpec((1536, 256), lambda i: (0, i)),
        compiler_params=pltpu.CompilerParams(vmem_limit_bytes=8 << 20),
        cost_estimate=pl.CostEstimate(flops=3 << 20, bytes_accessed=6 << 20, transcendentals=0),
    )(*pieces)


def turn_kernel(own, other, y_own, y_other, first, second, rows):
    col = lax.axis_index("col")
    place, core = col % 4, col % 2
    for piece, p in ((own, place), (other, place ^ 1), (y_own, place ^ 2), (y_other, place ^ 3)):
        rows[pl.ds(pl.multiple_of(p * 32, 32), 32), :] = piece[...]
    n = first.shape[0]
    tall = rows[...].T
    top, bottom = tall[:n], tall[n : 2 * n]
    first[...] = jnp.where(core == 0, top, bottom)
    second[...] = jnp.where(core == 0, bottom, top)


def turn(start, width, own, other, y_own, y_other, y_start):
    def part(first):
        return pl.BlockSpec((32, WIDE), lambda i: (0, first // WIDE))

    half = jax.ShapeDtypeStruct((width // 2, 128), F32)
    return pl.pallas_call(
        turn_kernel,
        grid=(1,),
        out_shape=[half, half],
        in_specs=[part(start)] * 2 + [part(y_start)] * 2,
        out_specs=[pl.BlockSpec((width // 2, 128), lambda i: (0, 0))] * 2,
        scratch_shapes=[pltpu.VMEM((128, WIDE), F32)],
        compiler_params=pltpu.CompilerParams(vmem_limit_bytes=8 << 20),
        cost_estimate=pl.CostEstimate(flops=1 << 20, bytes_accessed=2 << 20, transcendentals=0),
    )(own, other, y_own, y_other)


def product_kernel(own, far, opposite, near, own2, far2, opposite2, near2, amps, *rest):
    out, left = rest[-2:]
    steps = pl.num_programs(0) // 2

    def run(pieces):
        for k, piece in enumerate(pieces):
            high, low = split(piece[...])
            left[:, k * 128 : k * 128 + 128] = high
            left[:, k * 128 + 512 : k * 128 + 640] = low
            left[:, k * 128 + 1024 : k * 128 + 1152] = high
        out[...] = jnp.dot(left[...], amps[...], preferred_element_type=F32)

    @pl.when(pl.program_id(0) < steps)
    def _():
        run((own, far, opposite, near))

    @pl.when(pl.program_id(0) >= steps)
    def _():
        run((own2, far2, opposite2, near2))


def cut_kernel(own, other, right, left_, far, right_o, left_o, far_o, y, y_o, amps, *rest):
    out, rows, left = rest[-3:]
    col = lax.axis_index("col")
    y_hi, core = col // 2 % 2, col % 2

    def put(value, slot, y_side, c):
        rows[pl.ds(pl.multiple_of(slot * 128 + y_side * 64 + c * 32, 32), 32), :] = value

    from_left = jnp.where(core == 0, 3, 1)
    from_right = jnp.where(core == 0, 1, 3)
    for c, parts in ((core, (own, right, left_, far)), (1 - core, (other, right_o, left_o, far_o))):
        for part, slot in zip(parts, (0, from_left, from_right, 2)):
            put(part[...], slot, y_hi, c)
    for c, part in ((core, y), (1 - core, y_o)):
        for k, slot in enumerate((0, from_left, from_right, 2)):
            put(part[k * 32 : k * 32 + 32], slot, 1 - y_hi, c)
    high, low = split(rows[...].T)
    left[:, :512] = high
    left[:, 512:1024] = low
    left[:, 1024:] = high
    out[...] = jnp.dot(left[...], amps[...], preferred_element_type=F32)


def product_cut(pieces, amps, shape, before):
    in_specs = [pl.BlockSpec((min(p.shape[0], 128), 256), lambda i: (0, i)) for p in pieces]
    in_specs.append(pl.BlockSpec(memory_space=pltpu.VMEM))
    operands = [*pieces, amps]
    aliases = {}
    if before is not None:
        aliases = {len(operands): 0}
        in_specs.append(pl.BlockSpec(memory_space=pl.ANY))
        operands.append(before)
    return pl.pallas_call(
        cut_kernel,
        grid=(WIDE // 256,),
        out_shape=jax.ShapeDtypeStruct(shape, F32),
        in_specs=in_specs,
        out_specs=pl.BlockSpec((256, shape[1]), lambda i: (i, 0)),
        scratch_shapes=[pltpu.VMEM((512, 256), F32), pltpu.VMEM((256, 1536), BF)],
        input_output_aliases=aliases,
        compiler_params=pltpu.CompilerParams(vmem_limit_bytes=20 << 20),
        cost_estimate=pl.CostEstimate(flops=2 * WIDE * 1536 * shape[1], bytes_accessed=4 * WIDE * shape[1], transcendentals=0),
    )(*operands)


def product(start, width, tile, pieces, amps, shape, before):
    first, steps = start // tile, width // tile

    def rows(i):
        core = lax.axis_index("col") % 2
        return first + (i + core * (steps // 2)) % steps, 0

    in_specs = [pl.BlockSpec((tile, 128), lambda i: (jnp.minimum(i, steps // 2 - 1), 0))] * 4
    in_specs += [pl.BlockSpec((tile, 128), lambda i: (jnp.maximum(i - steps // 2, 0), 0))] * 4
    in_specs.append(pl.BlockSpec(memory_space=pltpu.VMEM))
    operands = [*pieces, amps]
    aliases = {}
    if before is not None:
        aliases = {len(operands): 0}
        in_specs.append(pl.BlockSpec(memory_space=pl.ANY))
        operands.append(before)
    return pl.pallas_call(
        product_kernel,
        grid=(steps,),
        out_shape=jax.ShapeDtypeStruct(shape, F32),
        in_specs=in_specs,
        out_specs=pl.BlockSpec((tile, shape[1]), rows),
        scratch_shapes=[pltpu.VMEM((tile, 1536), BF)],
        input_output_aliases=aliases,
        compiler_params=pltpu.CompilerParams(vmem_limit_bytes=20 << 20),
        cost_estimate=pl.CostEstimate(flops=2 * width * 1536 * shape[1], bytes_accessed=4 * width * shape[1], transcendentals=0),
    )(*operands)


def body(amplitudes, integrals):
    shape = (integrals.shape[1], amplitudes.shape[1])
    v, a = integrals, amplitudes
    ao, za, ya = swap_core(a), shift_z(a), swap_y_lo(a)
    zb, zy, yo = shift_z(ao), shift_z(ya), swap_core(ya)
    z2, y2, zz, zf = shift_z(za), shift_z(zy), shift_z(yo), swap_core(zb)
    zg = swap_core(zz)
    amps_in = (a, za, zf, z2, ya, zy, zg, y2)
    other = swap_core(v)
    v_cut, v0, rest = v[:, :WIDE], v[:, WIDE : 2 * WIDE], v[:, 2 * WIDE :]
    y0, y1 = swap_y_hi(v0), swap_y_hi(rest)
    cut = [send_x(v_cut, 1), send_x(v_cut, -1), send_x(v_cut, 2)]
    y_cut = swap_y_hi(jnp.concatenate([v_cut, *cut], 0))
    t0 = turn(WIDE, 1280, v, other, y0, swap_core(y0), 0)
    y1_other = swap_core(y1)
    t1, t2 = [turn(s, w, v, other, y1, y1_other, s - 2 * WIDE) for s, w, _ in CHUNKS[1:]]
    near0 = [shift_x(t) for t in t0]
    o0 = shift_x(near0[0])
    near1 = [shift_x(t) for t in t1] if EARLY else None
    amps_in, cut, y_cut, near0, o0, near1, t1, t2 = lax.optimization_barrier((amps_in, cut, y_cut, near0, o0, near1, t1, t2))
    if not EARLY:
        near1 = [shift_x(t) for t in t1]
    amps = stack_amps(amps_in)
    near2 = [shift_x(t) for t in t2]
    o1 = shift_x(near1[0])
    o2 = shift_x(near2[0])
    work = [(t0, near0, o0), (t1, near1, o1), (t2, near2, o2)]
    out = None
    for j, (start, width, tile) in enumerate(CHUNKS):
        if j == CUT_AT:
            cut_other = [swap_core(p) for p in cut]
            out = product_cut((v, other, *cut, *cut_other, y_cut, swap_core(y_cut)), amps, shape, out)
        (f, s), (near_f, near_s), o = work[j]
        pieces = (f, swap_core(near_s), o, near_f, s, swap_core(near_f), swap_core(o), near_s)
        out = product(start, width, tile, pieces, amps, shape, out)
    return out


def solution(mesh):
    in_specs = (P("row", "col"), P("col", "row"))
    out_specs = P("row", "col")
    return jax.shard_map(body, mesh=mesh, in_specs=in_specs, out_specs=out_specs, check_vma=False)
```

time: 227 us -> 92.7 us (0.41)
  waiting for transfers between devices: 129 us -> 9.63 us
  matrix products: 84.5 us -> 0 us
  starting transfers between devices: 0.04 us -> 47.8 us
  Pallas kernels: 0 us -> 30.8 us
  between operations: 13.4 us -> 0.12 us
  local copies, waits for them, and re-layouts: 0 us -> 4.12 us
    all_gather x2 -> x0, waiting for transfers between devices: 128 us -> none  [the longest x1 85.5 us: ladder(): lax.all_gather(integral_block, 'col', axis=0, tiled=True)]
    dot_general x1 -> x0, matrix products: 84.5 us -> none  [contract_rows(): lax.dot_general(left_block, right_block, (((0,), (0,)), ((), ())), precis...]
    ppermute x0 -> x42, starting transfers between devices: none -> 47.8 us  [the longest x6 14.1 us: shift_z(): return lax.ppermute(v, ('row', 'col'), pairs)]
    pallas_call x0 -> x8, Pallas kernels: none -> 30.8 us  [the longest x3 20.1 us: product(): pl.pallas_call(product_kernel, grid=(steps,), out_shape=jax.ShapeDtypeStr...]
    ppermute x0 -> x42, waiting for transfers between devices: none -> 9.63 us  [the longest x20 3.31 us: swap_core(): return lax.ppermute(v, 'col', [(i, i ^ 1) for i in range(16)])]
  transfers between devices with their start and end apart: 2 -> 42, of which waited for: 2 -> 7; matrix products, arithmetic and copies ran while one was open for 0% -> 1% of each run, Pallas kernels for 0% -> 27%
where the time goes in v1:
time: 92.7 us; the launch traced here: 92.4 us
  starting transfers between devices  47.8 us (52%)
  Pallas kernels  30.8 us (33%)
  waiting for transfers between devices  9.63 us (10%)
  local copies, waits for them, and re-layouts  4.12 us (4%)
    pallas_call x3, Pallas kernels, product(): pl.pallas_call(product_kernel, grid=(steps,), out_shape=jax.ShapeDtypeStr...  20.1 us
    ppermute x6, starting transfers between devices, shift_z(): return lax.ppermute(v, ('row', 'col'), pairs)  14.1 us
    ppermute x9, starting transfers between devices, shift_x(): lax.ppermute(v, 'col', [(i, (i + (4 if i % 2 == 0 else 12)) % 16) for i i...  12.7 us
    ppermute x20, starting transfers between devices, swap_core(): return lax.ppermute(v, 'col', [(i, i ^ 1) for i in range(16)])  12.3 us
    pallas_call x1, Pallas kernels, product_cut(): pl.pallas_call(cut_kernel, grid=(WIDE // 256,), out_shape=jax.ShapeDtypeS...  8.23 us
    ppermute x3, starting transfers between devices, send_x(): return lax.ppermute(v, 'col', [(i, (i + 4 * d) % 16) for i in range(16)])  4.28 us
    ppermute x3, starting transfers between devices, swap_y_hi(): return lax.ppermute(v, 'col', [(i, i ^ 2) for i in range(16)])  3.93 us
    ppermute x20, waiting for transfers between devices, swap_core(): return lax.ppermute(v, 'col', [(i, i ^ 1) for i in range(16)])  3.31 us
  transfers between devices with their start and end apart: 42, of which 7 were waited for; matrix products, arithmetic and copies ran while one was open for 1% of the time, Pallas kernels for 27%

profile of v1, /device:TPU:1, one launch (start us, length us, event | category | flops | bytes accessed | tf_op | source)
XLA Modules:
  0.0 92.4 jit_solution(17301755511551845829)
XLA Ops:
  0.0 1.1 %slice.11 = f32[32,2240]{1,0:T(8,128)S(1)} slice(f32[32,4800]{1,0:T(8,128)} %own.8), slice={[0:32], [2560:4800]} | slice | bytes 573440 | tf_op jit(solution)/shard_map/slice | solution.py:216
  1.1 3.8 %collective-permute-start.21 = (f32[32,2240]{1,0:T(8,128)S(1)}, f32[32,2240]{1,0:T(8,128)S(1)}, u32[]{:S(2)}, u32[]{:S(2)}) collective-permute-start(f32[32,2240]{1,0:T(8,128)S(1)} %slice.11), channel_id=1, source_target_pairs={{0,2},{1,3},{2,0},{3,1},{4,6},{5,7},{6,4},{7,5},{8,10},{9,11},{10,... | collective-permute-start | bytes 860168 | tf_op jit(solution)/shard_map/ppermute | solution.py:21
  4.9 1.0 %fusion = (f32[32,1280]{1,0:T(8,128)S(1)}, f32[32,1280]{1,0:T(8,128)S(1)}) fusion(f32[32,4800]{1,0:T(8,128)} %own.8), kind=kLoop, calls=%fused_computation.1 | loop fusion | bytes 655360 | tf_op jit(solution)/shard_map/slice | solution.py:216
  5.9 1.3 %collective-permute-start.11 = (f32[32,1280]{1,0:T(8,128)S(1)}, f32[32,1280]{1,0:T(8,128)S(1)}, u32[]{:S(2)}, u32[]{:S(2)}) collective-permute-start(f32[32,1280]{1,0:T(8,128)S(1)} %get-tuple-element.56), channel_id=1, source_target_pairs={{0,4},{1,5},{2,6},{3,7},{4,8},{5,9},{6,10},{7,11},{8,12},{9,13},{1... | collective-permute-start | bytes 491528 | tf_op jit(solution)/shard_map/ppermute | solution.py:33
  7.2 1.5 %collective-permute-start.12 = (f32[32,1280]{1,0:T(8,128)S(1)}, f32[32,1280]{1,0:T(8,128)S(1)}, u32[]{:S(2)}, u32[]{:S(2)}) collective-permute-start(f32[32,1280]{1,0:T(8,128)S(1)} %get-tuple-element.56), channel_id=1, source_target_pairs={{0,12},{1,13},{2,14},{3,15},{4,0},{5,1},{6,2},{7,3},{8,4},{9,5},{1... | collective-permute-start | bytes 491528 | tf_op jit(solution)/shard_map/ppermute | solution.py:33
  8.6 1.5 %collective-permute-start.13 = (f32[32,1280]{1,0:T(8,128)S(1)}, f32[32,1280]{1,0:T(8,128)S(1)}, u32[]{:S(2)}, u32[]{:S(2)}) collective-permute-start(f32[32,1280]{1,0:T(8,128)S(1)} %get-tuple-element.56), channel_id=1, source_target_pairs={{0,8},{1,9},{2,10},{3,11},{4,12},{5,13},{6,14},{7,15},{8,0},{9,1},... | collective-permute-start | bytes 491528 | tf_op jit(solution)/shard_map/ppermute | solution.py:33
  10.2 0.1 collective-permute-start.16
  10.2 1.7 %collective-permute-done.11.right = f32[32,1280]{1,0:T(8,128)S(1)} collective-permute-done((f32[32,1280]{1,0:T(8,128)S(1)}, f32[32,1280]{1,0:T(8,128)S(1)}, u32[]{:S(2)}, u32[]{:S(2)}) %collective-permute-start.11) | collective-permute-done | bytes 163872 | tf_op jit(solution)/shard_map/ppermute | solution.py:33
  11.9 0.4 collective-permute-start.5
  12.3 0.0 collective-permute-done.12.left_
  12.3 3.8 %collective-permute-start = (f32[64,1280]{1,0:T(8,128)}, f32[64,1280]{1,0:T(8,128)S(1)}, u32[]{:S(2)}, u32[]{:S(2)}) collective-permute-start(f32[64,1280]{1,0:T(8,128)} %own.7), channel_id=1, source_target_pairs={{0,16},{1,49},{2,18},{3,51},{4,20},{5,53},{6,22},{7,55},{8,24},{9,... | collective-permute-start | bytes 983048 | tf_op jit(solution)/shard_map/ppermute | solution.py:42
  16.1 0.3 collective-permute-done.13.far
  16.4 2.1 %collective-permute-start.1 = (f32[64,1280]{1,0:T(8,128)}, f32[64,1280]{1,0:T(8,128)S(1)}, u32[]{:S(2)}, u32[]{:S(2)}) collective-permute-start(f32[64,1280]{1,0:T(8,128)} %own.7), channel_id=1, source_target_pairs={{0,1},{1,0},{2,3},{3,2},{4,5},{5,4},{6,7},{7,6},{8,9},{9,8},{10,11... | collective-permute-start | bytes 983048 | tf_op jit(solution)/shard_map/ppermute | solution.py:17
  18.5 0.0 collective-permute-done.16.y_own
  18.5 2.1 %collective-permute-start.15 = (f32[32,4800]{1,0:T(8,128)}, f32[32,4800]{1,0:T(8,128)S(1)}, u32[]{:S(2)}, u32[]{:S(2)}) collective-permute-start(f32[32,4800]{1,0:T(8,128)} %own.8), channel_id=1, source_target_pairs={{0,1},{1,0},{2,3},{3,2},{4,5},{5,4},{6,7},{7,6},{8,9},{9,8},{10,11... | collective-permute-start | bytes 1843208 | tf_op jit(solution)/shard_map/ppermute | solution.py:17
  20.6 0.0 collective-permute-done.21.y_own
  20.6 0.0 collective-permute-start.17
  20.7 1.7 %collective-permute-done.17.y_other = f32[32,1280]{1,0:T(8,128)S(1)} collective-permute-done((f32[32,1280]{1,0:T(8,128)S(1)}, f32[32,1280]{1,0:T(8,128)S(1)}, u32[]{:S(2)}, u32[]{:S(2)}) %collective-permute-start.17) | collective-permute-done | bytes 163872 | tf_op jit(solution)/shard_map/ppermute | solution.py:17
  22.4 0.1 collective-permute-start.14
  22.5 3.8 %collective-permute-start.6 = (f32[64,1280]{1,0:T(8,128)S(1)}, f32[64,1280]{1,0:T(8,128)S(1)}, u32[]{:S(2)}, u32[]{:S(2)}) collective-permute-start(f32[64,1280]{1,0:T(8,128)S(1)} %collective-permute-done.5.y_own), channel_id=1, source_target_pairs={{0,16},{1,49},{2,18},{3,51},{4,20},{5,53},{6,22},{7,55},{8,24},{9,... | collective-permute-start | bytes 983048 | tf_op jit(solution)/shard_map/ppermute | solution.py:42
  26.2 0.0 collective-permute-done.near
  26.2 0.0 collective-permute-start.7
  26.2 0.5 collective-permute-start.22
  26.7 1.5 %collective-permute-done.22.y_other = f32[32,2240]{1,0:T(8,128)S(1)} collective-permute-done((f32[32,2240]{1,0:T(8,128)S(1)}, f32[32,2240]{1,0:T(8,128)S(1)}, u32[]{:S(2)}, u32[]{:S(2)}) %collective-permute-start.22) | collective-permute-done | bytes 286752 | tf_op jit(solution)/shard_map/ppermute | solution.py:17
  28.3 1.2 %collective-permute-start.4 = (f32[64,1280]{1,0:T(8,128)S(1)}, f32[64,1280]{1,0:T(8,128)S(1)}, u32[]{:S(2)}, u32[]{:S(2)}) collective-permute-start(f32[64,1280]{1,0:T(8,128)S(1)} %collective-permute-done.near), channel_id=1, source_target_pairs={{0,16},{1,49},{2,18},{3,51},{4,20},{5,53},{6,22},{7,55},{8,24},{9,... | collective-permute-start | bytes 983048 | tf_op jit(solution)/shard_map/ppermute | solution.py:42
  29.5 1.7 %collective-permute-start.2 = (f32[64,1280]{1,0:T(8,128)S(1)}, f32[64,1280]{1,0:T(8,128)S(1)}, u32[]{:S(2)}, u32[]{:S(2)}) collective-permute-start(f32[64,1280]{1,0:T(8,128)S(1)} %collective-permute-done.1), channel_id=1, source_target_pairs={{0,16},{1,49},{2,18},{3,51},{4,20},{5,53},{6,22},{7,55},{8,24},{9,... | collective-permute-start | bytes 983048 | tf_op jit(solution)/shard_map/ppermute | solution.py:42
  31.2 1.1 %copy-done = f32[32,4800]{1,0:T(8,128)S(1)} copy-done((f32[32,4800]{1,0:T(8,128)S(1)}, f32[32,4800]{1,0:T(8,128)}, u32[]{:S(2)}) %copy-start) | copy-done | bytes 614424
  32.3 0.3 shard_map.28
  32.6 2.3 %collective-permute-start.18 = (f32[640,128]{1,0:T(8,128)S(1)}, f32[640,128]{1,0:T(8,128)S(1)}, u32[]{:S(2)}, u32[]{:S(2)}) collective-permute-start(f32[640,128]{1,0:T(8,128)S(1)} %get-tuple-element.30.own), channel_id=1, source_target_pairs={{0,4},{1,13},{2,6},{3,15},{4,8},{5,1},{6,10},{7,3},{8,12},{9,5},{1... | collective-permute-start | bytes 983048 | tf_op jit(solution)/shard_map/ppermute | solution.py:29
  34.9 1.0 %collective-permute-start.8 = (f32[64,1280]{1,0:T(8,128)S(1)}, f32[64,1280]{1,0:T(8,128)S(1)}, u32[]{:S(2)}, u32[]{:S(2)}) collective-permute-start(f32[64,1280]{1,0:T(8,128)S(1)} %collective-permute-done.7), channel_id=1, source_target_pairs={{0,16},{1,49},{2,18},{3,51},{4,20},{5,53},{6,22},{7,55},{8,24},{9,... | collective-permute-start | bytes 983048 | tf_op jit(solution)/shard_map/ppermute | solution.py:42
  35.9 1.3 %collective-permute-start.19 = (f32[640,128]{1,0:T(8,128)S(1)}, f32[640,128]{1,0:T(8,128)S(1)}, u32[]{:S(2)}, u32[]{:S(2)}) collective-permute-start(f32[640,128]{1,0:T(8,128)S(1)} %get-tuple-element.31.own2), channel_id=1, source_target_pairs={{0,4},{1,13},{2,6},{3,15},{4,8},{5,1},{6,10},{7,3},{8,12},{9,5},{1... | collective-permute-start | bytes 983048 | tf_op jit(solution)/shard_map/ppermute | solution.py:29
  37.2 0.8 collective-permute-done.2
  38.0 2.7 %collective-permute-start.10 = (f32[64,1280]{1,0:T(8,128)S(1)}, f32[64,1280]{1,0:T(8,128)S(1)}, u32[]{:S(2)}, u32[]{:S(2)}) collective-permute-start(f32[64,1280]{1,0:T(8,128)S(1)} %collective-permute-done.6.y_near), channel_id=1, source_target_pairs={{0,16},{1,49},{2,18},{3,51},{4,20},{5,53},{6,22},{7,55},{8,24},{9,... | collective-permute-start | bytes 983048 | tf_op jit(solution)/shard_map/ppermute | solution.py:42
  40.7 0.4 collective-permute-start.3
  41.1 2.7 %collective-permute-start.20 = (f32[640,128]{1,0:T(8,128)S(1)}, f32[640,128]{1,0:T(8,128)S(1)}, u32[]{:S(2)}, u32[]{:S(2)}) collective-permute-start(f32[640,128]{1,0:T(8,128)S(1)} %collective-permute-done.18.near), channel_id=1, source_target_pairs={{0,4},{1,13},{2,6},{3,15},{4,8},{5,1},{6,10},{7,3},{8,12},{9,5},{1... | collective-permute-start | bytes 983048 | tf_op jit(solution)/shard_map/ppermute | solution.py:29
  43.7 0.3 shard_map.29
  44.0 0.3 shard_map.30
  44.3 0.7 collective-permute-done.10.y_opposite
  45.0 2.7 %collective-permute-done.20.opposite = f32[640,128]{1,0:T(8,128)S(1)} collective-permute-done((f32[640,128]{1,0:T(8,128)S(1)}, f32[640,128]{1,0:T(8,128)S(1)}, u32[]{:S(2)}, u32[]{:S(2)}) %collective-permute-start.20) | collective-permute-done | bytes 327712 | tf_op jit(solution)/shard_map/ppermute | solution.py:29
  47.8 1.9 %collective-permute-start.35 = (f32[32,1280]{1,0:T(8,128)S(1)}, f32[32,1280]{1,0:T(8,128)S(1)}, u32[]{:S(2)}, u32[]{:S(2)}) collective-permute-start(f32[32,1280]{1,0:T(8,128)S(1)} %collective-permute-done.11.right), channel_id=1, source_target_pairs={{0,1},{1,0},{2,3},{3,2},{4,5},{5,4},{6,7},{7,6},{8,9},{9,8},{10,11... | collective-permute-start | bytes 491528 | tf_op jit(solution)/shard_map/ppermute | solution.py:17
  49.7 0.0 collective-permute-start.36
  49.7 0.5 collective-permute-start.39
  50.2 0.0 collective-permute-start.40
  50.2 0.5 collective-permute-start.41
  50.7 0.0 collective-permute-done.35.right_o
  50.7 1.8 %collective-permute-start.31 = (f32[640,128]{1,0:T(8,128)S(1)}, f32[640,128]{1,0:T(8,128)S(1)}, u32[]{:S(2)}, u32[]{:S(2)}) collective-permute-start(f32[640,128]{1,0:T(8,128)S(1)} %get-tuple-element.46.own), channel_id=1, source_target_pairs={{0,4},{1,13},{2,6},{3,15},{4,8},{5,1},{6,10},{7,3},{8,12},{9,5},{1... | collective-permute-start | bytes 983048 | tf_op jit(solution)/shard_map/ppermute | solution.py:29
  52.6 1.0 %copy-done.2 = f32[64,1280]{1,0:T(8,128)S(1)} copy-done((f32[64,1280]{1,0:T(8,128)S(1)}, f32[64,1280]{1,0:T(8,128)}, u32[]{:S(2)}) %copy-start.2) | copy-done | bytes 327704
  53.5 1.5 %shard_map.31.amps = bf16[1536,1280]{1,0:T(8,128)(2,1)S(1)} custom-call(f32[64,1280]{1,0:T(8,128)S(1)} %copy-done.2, f32[64,1280]{1,0:T(8,128)S(1)} %collective-permute-done.near, f32[64,1280]{1,0:T(8,128)S(1)} %collective-permute-done.3.far, f32[64,1280]{1,0:T(8,128)S(1)} %collective-permute-done.4.opposite, f32[64,1280]{1,0:T(8,128)S(1)} %collective-permute-done.5.y_own, ...), custom_call_target="tpu_custom_call" | custom-call | flops 3145728 | bytes 6291456 | tf_op jit(solution)/shard_map/pallas_call | solution.py:72
  55.1 0.6 collective-permute-start.37
  55.6 1.1 %collective-permute-start.29 = (f32[640,128]{1,0:T(8,128)S(1)}, f32[640,128]{1,0:T(8,128)S(1)}, u32[]{:S(2)}, u32[]{:S(2)}) collective-permute-start(f32[640,128]{1,0:T(8,128)S(1)} %get-tuple-element.47.own2), channel_id=1, source_target_pairs={{0,4},{1,13},{2,6},{3,15},{4,8},{5,1},{6,10},{7,3},{8,12},{9,5},{1... | collective-permute-start | bytes 983048 | tf_op jit(solution)/shard_map/ppermute | solution.py:29
  56.7 0.6 collective-permute-start.25
  57.3 2.3 %collective-permute-start.32 = (f32[640,128]{1,0:T(8,128)S(1)}, f32[640,128]{1,0:T(8,128)S(1)}, u32[]{:S(2)}, u32[]{:S(2)}) collective-permute-start(f32[640,128]{1,0:T(8,128)S(1)} %collective-permute-done.31.near), channel_id=1, source_target_pairs={{0,4},{1,13},{2,6},{3,15},{4,8},{5,1},{6,10},{7,3},{8,12},{9,5},{1... | collective-permute-start | bytes 983048 | tf_op jit(solution)/shard_map/ppermute | solution.py:29
  59.7 7.1 %shard_map.32.rest_0_ = f32[4800,1280]{1,0:T(8,128)} custom-call(f32[640,128]{1,0:T(8,128)S(1)} %get-tuple-element.30.own, f32[640,128]{1,0:T(8,128)S(1)} %collective-permute-done.39.far, f32[640,128]{1,0:T(8,128)S(1)} %collective-permute-done.20.opposite, f32[640,128]{1,0:T(8,128)S(1)} %collective-permute-done.18.near, ...), custom_call_target="tpu_custom_call" | custom-call | flops 5033164800 | bytes 6553600 | tf_op jit(solution)/shard_map/pallas_call | solution.py:194
  66.8 0.0 collective-permute-start.23
  66.8 0.6 collective-permute-start.26
  67.4 1.4 %collective-permute-start.33 = (f32[640,128]{1,0:T(8,128)S(1)}, f32[640,128]{1,0:T(8,128)S(1)}, u32[]{:S(2)}, u32[]{:S(2)}) collective-permute-start(f32[640,128]{1,0:T(8,128)S(1)} %collective-permute-done.31.near), channel_id=1, source_target_pairs={{0,1},{1,0},{2,3},{3,2},{4,5},{5,4},{6,7},{7,6},{8,9},{9,8},{10,11... | collective-permute-start | bytes 983048 | tf_op jit(solution)/shard_map/ppermute | solution.py:17
  68.8 1.3 %collective-permute-start.30 = (f32[640,128]{1,0:T(8,128)S(1)}, f32[640,128]{1,0:T(8,128)S(1)}, u32[]{:S(2)}, u32[]{:S(2)}) collective-permute-start(f32[640,128]{1,0:T(8,128)S(1)} %collective-permute-done.29.near2), channel_id=1, source_target_pairs={{0,1},{1,0},{2,3},{3,2},{4,5},{5,4},{6,7},{7,6},{8,9},{9,8},{10,11... | collective-permute-start | bytes 983048 | tf_op jit(solution)/shard_map/ppermute | solution.py:17
  70.2 0.0 collective-permute-start.34
  70.2 8.2 %shard_map.33.rest_0_ = f32[4800,1280]{1,0:T(8,128)} custom-call(f32[32,4800]{1,0:T(8,128)S(1)} %copy-done.1, f32[32,4800]{1,0:T(8,128)S(1)} %collective-permute-done.15.other, f32[32,1280]{1,0:T(8,128)S(1)} %collective-permute-done.11.right, f32[32,1280]{1,0:T(8,128)S(1)} %collective-permute-done.12.left_, ...), custom_call_target="tpu_custom_call", output_to_operand_aliasing={{}: (11, {})} | custom-call | flops 5033164800 | bytes 6553600 | tf_op jit(solution)/shard_map/pallas_call | solution.py:165
  78.4 0.5 collective-permute-start.27
  78.9 0.1 collective-permute-start.24
  79.0 0.4 collective-permute-start.28
  79.4 7.2 %shard_map.34.rest_0_ = f32[4800,1280]{1,0:T(8,128)} custom-call(f32[640,128]{1,0:T(8,128)S(1)} %get-tuple-element.46.own, f32[640,128]{1,0:T(8,128)S(1)} %collective-permute-done.30.far, f32[640,128]{1,0:T(8,128)S(1)} %collective-permute-done.32.opposite, f32[640,128]{1,0:T(8,128)S(1)} %collective-permute-done.31.near, ...), custom_call_target="tpu_custom_call", output_to_operand_aliasing={{}: (9, {})} | custom-call | flops 5033164800 | bytes 6553600 | tf_op jit(solution)/shard_map/pallas_call | solution.py:194
  86.6 5.8 %shard_map.35 = f32[4800,1280]{1,0:T(8,128)} custom-call(f32[480,128]{1,0:T(8,128)S(1)} %get-tuple-element.36.own, f32[480,128]{1,0:T(8,128)S(1)} %collective-permute-done.24.far, f32[480,128]{1,0:T(8,128)S(1)} %collective-permute-done.26.opposite, f32[480,128]{1,0:T(8,128)S(1)} %collective-permute-done.25.near, ...), custom_call_target="tpu_custom_call", output_to_operand_aliasing={{}: (9, {})} | custom-call | flops 3774873600 | bytes 4915200 | tf_op jit(solution)/shard_map/pallas_call | solution.py:194
  (37 shorter events, 0.1 us)
Async XLA Ops:
  0.0 70.2 %copy-start.1 = (f32[32,4800]{1,0:T(8,128)S(1)}, f32[32,4800]{1,0:T(8,128)}, u32[]{:S(2)}) copy-start(f32[32,4800]{1,0:T(8,128)} %own.8) | copy-start | bytes 1843204
  1.1 19.6 %collective-permute-start.21 = (f32[32,2240]{1,0:T(8,128)S(1)}, f32[32,2240]{1,0:T(8,128)S(1)}, u32[]{:S(2)}, u32[]{:S(2)}) collective-permute-start(f32[32,2240]{1,0:T(8,128)S(1)} %slice.11), channel_id=1, source_target_pairs={{0,2},{1,3},{2,0},{3,1},{4,6},{5,7},{6,4},{7,5},{8,10},{9,11},{10,... | collective-permute-start | bytes 860168 | tf_op jit(solution)/shard_map/ppermute | solution.py:21
  5.9 6.0 %collective-permute-start.11 = (f32[32,1280]{1,0:T(8,128)S(1)}, f32[32,1280]{1,0:T(8,128)S(1)}, u32[]{:S(2)}, u32[]{:S(2)}) collective-permute-start(f32[32,1280]{1,0:T(8,128)S(1)} %get-tuple-element.56), channel_id=1, source_target_pairs={{0,4},{1,5},{2,6},{3,7},{4,8},{5,9},{6,10},{7,11},{8,12},{9,13},{1... | collective-permute-start | bytes 491528 | tf_op jit(solution)/shard_map/ppermute | solution.py:33
  7.2 5.1 %collective-permute-start.12 = (f32[32,1280]{1,0:T(8,128)S(1)}, f32[32,1280]{1,0:T(8,128)S(1)}, u32[]{:S(2)}, u32[]{:S(2)}) collective-permute-start(f32[32,1280]{1,0:T(8,128)S(1)} %get-tuple-element.56), channel_id=1, source_target_pairs={{0,12},{1,13},{2,14},{3,15},{4,0},{5,1},{6,2},{7,3},{8,4},{9,5},{1... | collective-permute-start | bytes 491528 | tf_op jit(solution)/shard_map/ppermute | solution.py:33
  8.6 7.8 %collective-permute-start.13 = (f32[32,1280]{1,0:T(8,128)S(1)}, f32[32,1280]{1,0:T(8,128)S(1)}, u32[]{:S(2)}, u32[]{:S(2)}) collective-permute-start(f32[32,1280]{1,0:T(8,128)S(1)} %get-tuple-element.56), channel_id=1, source_target_pairs={{0,8},{1,9},{2,10},{3,11},{4,12},{5,13},{6,14},{7,15},{8,0},{9,1},... | collective-permute-start | bytes 491528 | tf_op jit(solution)/shard_map/ppermute | solution.py:33
  10.2 8.3 %collective-permute-start.16 = (f32[32,1280]{1,0:T(8,128)S(1)}, f32[32,1280]{1,0:T(8,128)S(1)}, u32[]{:S(2)}, u32[]{:S(2)}) collective-permute-start(f32[32,1280]{1,0:T(8,128)S(1)} %get-tuple-element.55), channel_id=1, source_target_pairs={{0,2},{1,3},{2,0},{3,1},{4,6},{5,7},{6,4},{7,5},{8,10},{9,11},{10,... | collective-permute-start | bytes 491528 | tf_op jit(solution)/shard_map/ppermute | solution.py:21
  11.9 10.5 %collective-permute-start.5 = (f32[64,1280]{1,0:T(8,128)}, f32[64,1280]{1,0:T(8,128)S(1)}, u32[]{:S(2)}, u32[]{:S(2)}) collective-permute-start(f32[64,1280]{1,0:T(8,128)} %own.7), channel_id=1, source_target_pairs={{0,64},{16,80},{32,96},{48,112},{64,0},{80,16},{96,32},{112,48},{1... | collective-permute-start | bytes 983048 | tf_op jit(solution)/shard_map/ppermute | solution.py:25
  12.3 13.9 %collective-permute-start = (f32[64,1280]{1,0:T(8,128)}, f32[64,1280]{1,0:T(8,128)S(1)}, u32[]{:S(2)}, u32[]{:S(2)}) collective-permute-start(f32[64,1280]{1,0:T(8,128)} %own.7), channel_id=1, source_target_pairs={{0,16},{1,49},{2,18},{3,51},{4,20},{5,53},{6,22},{7,55},{8,24},{9,... | collective-permute-start | bytes 983048 | tf_op jit(solution)/shard_map/ppermute | solution.py:42
  16.4 9.8 %collective-permute-start.1 = (f32[64,1280]{1,0:T(8,128)}, f32[64,1280]{1,0:T(8,128)S(1)}, u32[]{:S(2)}, u32[]{:S(2)}) collective-permute-start(f32[64,1280]{1,0:T(8,128)} %own.7), channel_id=1, source_target_pairs={{0,1},{1,0},{2,3},{3,2},{4,5},{5,4},{6,7},{7,6},{8,9},{9,8},{10,11... | collective-permute-start | bytes 983048 | tf_op jit(solution)/shard_map/ppermute | solution.py:17
  18.5 10.9 %collective-permute-start.15 = (f32[32,4800]{1,0:T(8,128)}, f32[32,4800]{1,0:T(8,128)S(1)}, u32[]{:S(2)}, u32[]{:S(2)}) collective-permute-start(f32[32,4800]{1,0:T(8,128)} %own.8), channel_id=1, source_target_pairs={{0,1},{1,0},{2,3},{3,2},{4,5},{5,4},{6,7},{7,6},{8,9},{9,8},{10,11... | collective-permute-start | bytes 1843208 | tf_op jit(solution)/shard_map/ppermute | solution.py:17
  20.6 1.8 %collective-permute-start.17 = (f32[32,1280]{1,0:T(8,128)S(1)}, f32[32,1280]{1,0:T(8,128)S(1)}, u32[]{:S(2)}, u32[]{:S(2)}) collective-permute-start(f32[32,1280]{1,0:T(8,128)S(1)} %collective-permute-done.16.y_own), channel_id=1, source_target_pairs={{0,1},{1,0},{2,3},{3,2},{4,5},{5,4},{6,7},{7,6},{8,9},{9,8},{10,11... | collective-permute-start | bytes 491528 | tf_op jit(solution)/shard_map/ppermute | solution.py:17
  22.4 18.3 %collective-permute-start.14 = (f32[128,1280]{1,0:T(8,128)S(1)}, f32[128,1280]{1,0:T(8,128)S(1)}, u32[]{:S(2)}, u32[]{:S(2)}) collective-permute-start(f32[128,1280]{1,0:T(8,128)S(1)} %pad_maximum_fusion), channel_id=1, source_target_pairs={{0,2},{1,3},{2,0},{3,1},{4,6},{5,7},{6,4},{7,5},{8,10},{9,11},{10,... | collective-permute-start | bytes 1966088 | tf_op jit(solution)/shard_map/ppermute | solution.py:21
  22.5 10.1 %collective-permute-start.6 = (f32[64,1280]{1,0:T(8,128)S(1)}, f32[64,1280]{1,0:T(8,128)S(1)}, u32[]{:S(2)}, u32[]{:S(2)}) collective-permute-start(f32[64,1280]{1,0:T(8,128)S(1)} %collective-permute-done.5.y_own), channel_id=1, source_target_pairs={{0,16},{1,49},{2,18},{3,51},{4,20},{5,53},{6,22},{7,55},{8,24},{9,... | collective-permute-start | bytes 983048 | tf_op jit(solution)/shard_map/ppermute | solution.py:42
  26.2 8.7 %collective-permute-start.7 = (f32[64,1280]{1,0:T(8,128)S(1)}, f32[64,1280]{1,0:T(8,128)S(1)}, u32[]{:S(2)}, u32[]{:S(2)}) collective-permute-start(f32[64,1280]{1,0:T(8,128)S(1)} %collective-permute-done.5.y_own), channel_id=1, source_target_pairs={{0,1},{1,0},{2,3},{3,2},{4,5},{5,4},{6,7},{7,6},{8,9},{9,8},{10,11... | collective-permute-start | bytes 983048 | tf_op jit(solution)/shard_map/ppermute | solution.py:17
  26.2 2.0 %collective-permute-start.22 = (f32[32,2240]{1,0:T(8,128)S(1)}, f32[32,2240]{1,0:T(8,128)S(1)}, u32[]{:S(2)}, u32[]{:S(2)}) collective-permute-start(f32[32,2240]{1,0:T(8,128)S(1)} %collective-permute-done.21.y_own), channel_id=1, source_target_pairs={{0,1},{1,0},{2,3},{3,2},{4,5},{5,4},{6,7},{7,6},{8,9},{9,8},{10,11... | collective-permute-start | bytes 860168 | tf_op jit(solution)/shard_map/ppermute | solution.py:17
  28.3 7.7 %collective-permute-start.4 = (f32[64,1280]{1,0:T(8,128)S(1)}, f32[64,1280]{1,0:T(8,128)S(1)}, u32[]{:S(2)}, u32[]{:S(2)}) collective-permute-start(f32[64,1280]{1,0:T(8,128)S(1)} %collective-permute-done.near), channel_id=1, source_target_pairs={{0,16},{1,49},{2,18},{3,51},{4,20},{5,53},{6,22},{7,55},{8,24},{9,... | collective-permute-start | bytes 983048 | tf_op jit(solution)/shard_map/ppermute | solution.py:42
  29.5 8.5 %collective-permute-start.2 = (f32[64,1280]{1,0:T(8,128)S(1)}, f32[64,1280]{1,0:T(8,128)S(1)}, u32[]{:S(2)}, u32[]{:S(2)}) collective-permute-start(f32[64,1280]{1,0:T(8,128)S(1)} %collective-permute-done.1), channel_id=1, source_target_pairs={{0,16},{1,49},{2,18},{3,51},{4,20},{5,53},{6,22},{7,55},{8,24},{9,... | collective-permute-start | bytes 983048 | tf_op jit(solution)/shard_map/ppermute | solution.py:42
  31.2 1.1 %copy-start = (f32[32,4800]{1,0:T(8,128)S(1)}, f32[32,4800]{1,0:T(8,128)}, u32[]{:S(2)}) copy-start(f32[32,4800]{1,0:T(8,128)} %own.8) | copy-start | bytes 1843204
  32.6 8.5 %collective-permute-start.18 = (f32[640,128]{1,0:T(8,128)S(1)}, f32[640,128]{1,0:T(8,128)S(1)}, u32[]{:S(2)}, u32[]{:S(2)}) collective-permute-start(f32[640,128]{1,0:T(8,128)S(1)} %get-tuple-element.30.own), channel_id=1, source_target_pairs={{0,4},{1,13},{2,6},{3,15},{4,8},{5,1},{6,10},{7,3},{8,12},{9,5},{1... | collective-permute-start | bytes 983048 | tf_op jit(solution)/shard_map/ppermute | solution.py:29
  34.9 8.8 %collective-permute-start.8 = (f32[64,1280]{1,0:T(8,128)S(1)}, f32[64,1280]{1,0:T(8,128)S(1)}, u32[]{:S(2)}, u32[]{:S(2)}) collective-permute-start(f32[64,1280]{1,0:T(8,128)S(1)} %collective-permute-done.7), channel_id=1, source_target_pairs={{0,16},{1,49},{2,18},{3,51},{4,20},{5,53},{6,22},{7,55},{8,24},{9,... | collective-permute-start | bytes 983048 | tf_op jit(solution)/shard_map/ppermute | solution.py:42
  35.9 8.4 %collective-permute-start.19 = (f32[640,128]{1,0:T(8,128)S(1)}, f32[640,128]{1,0:T(8,128)S(1)}, u32[]{:S(2)}, u32[]{:S(2)}) collective-permute-start(f32[640,128]{1,0:T(8,128)S(1)} %get-tuple-element.31.own2), channel_id=1, source_target_pairs={{0,4},{1,13},{2,6},{3,15},{4,8},{5,1},{6,10},{7,3},{8,12},{9,5},{1... | collective-permute-start | bytes 983048 | tf_op jit(solution)/shard_map/ppermute | solution.py:29
  38.0 7.0 %collective-permute-start.10 = (f32[64,1280]{1,0:T(8,128)S(1)}, f32[64,1280]{1,0:T(8,128)S(1)}, u32[]{:S(2)}, u32[]{:S(2)}) collective-permute-start(f32[64,1280]{1,0:T(8,128)S(1)} %collective-permute-done.6.y_near), channel_id=1, source_target_pairs={{0,16},{1,49},{2,18},{3,51},{4,20},{5,53},{6,22},{7,55},{8,24},{9,... | collective-permute-start | bytes 983048 | tf_op jit(solution)/shard_map/ppermute | solution.py:42
  40.7 4.4 %collective-permute-start.3 = (f32[64,1280]{1,0:T(8,128)S(1)}, f32[64,1280]{1,0:T(8,128)S(1)}, u32[]{:S(2)}, u32[]{:S(2)}) collective-permute-start(f32[64,1280]{1,0:T(8,128)S(1)} %collective-permute-done.2), channel_id=1, source_target_pairs={{0,1},{1,0},{2,3},{3,2},{4,5},{5,4},{6,7},{7,6},{8,9},{9,8},{10,11... | collective-permute-start | bytes 983048 | tf_op jit(solution)/shard_map/ppermute | solution.py:17
  41.1 6.7 %collective-permute-start.20 = (f32[640,128]{1,0:T(8,128)S(1)}, f32[640,128]{1,0:T(8,128)S(1)}, u32[]{:S(2)}, u32[]{:S(2)}) collective-permute-start(f32[640,128]{1,0:T(8,128)S(1)} %collective-permute-done.18.near), channel_id=1, source_target_pairs={{0,4},{1,13},{2,6},{3,15},{4,8},{5,1},{6,10},{7,3},{8,12},{9,5},{1... | collective-permute-start | bytes 983048 | tf_op jit(solution)/shard_map/ppermute | solution.py:29
  43.7 4.0 %collective-permute-start.9 = (f32[64,1280]{1,0:T(8,128)S(1)}, f32[64,1280]{1,0:T(8,128)S(1)}, u32[]{:S(2)}, u32[]{:S(2)}) collective-permute-start(f32[64,1280]{1,0:T(8,128)S(1)} %collective-permute-done.8), channel_id=1, source_target_pairs={{0,1},{1,0},{2,3},{3,2},{4,5},{5,4},{6,7},{7,6},{8,9},{9,8},{10,11... | collective-permute-start | bytes 983048 | tf_op jit(solution)/shard_map/ppermute | solution.py:17
  47.8 3.0 %collective-permute-start.35 = (f32[32,1280]{1,0:T(8,128)S(1)}, f32[32,1280]{1,0:T(8,128)S(1)}, u32[]{:S(2)}, u32[]{:S(2)}) collective-permute-start(f32[32,1280]{1,0:T(8,128)S(1)} %collective-permute-done.11.right), channel_id=1, source_target_pairs={{0,1},{1,0},{2,3},{3,2},{4,5},{5,4},{6,7},{7,6},{8,9},{9,8},{10,11... | collective-permute-start | bytes 491528 | tf_op jit(solution)/shard_map/ppermute | solution.py:17
  49.7 2.9 %collective-permute-start.36 = (f32[32,1280]{1,0:T(8,128)S(1)}, f32[32,1280]{1,0:T(8,128)S(1)}, u32[]{:S(2)}, u32[]{:S(2)}) collective-permute-start(f32[32,1280]{1,0:T(8,128)S(1)} %collective-permute-done.12.left_), channel_id=1, source_target_pairs={{0,1},{1,0},{2,3},{3,2},{4,5},{5,4},{6,7},{7,6},{8,9},{9,8},{10,11... | collective-permute-start | bytes 491528 | tf_op jit(solution)/shard_map/ppermute | solution.py:17
  49.7 5.4 %collective-permute-start.39 = (f32[640,128]{1,0:T(8,128)S(1)}, f32[640,128]{1,0:T(8,128)S(1)}, u32[]{:S(2)}, u32[]{:S(2)}) collective-permute-start(f32[640,128]{1,0:T(8,128)S(1)} %collective-permute-done.19.near2), channel_id=1, source_target_pairs={{0,1},{1,0},{2,3},{3,2},{4,5},{5,4},{6,7},{7,6},{8,9},{9,8},{10,11... | collective-permute-start | bytes 983048 | tf_op jit(solution)/shard_map/ppermute | solution.py:17
  50.2 5.4 %collective-permute-start.40 = (f32[640,128]{1,0:T(8,128)S(1)}, f32[640,128]{1,0:T(8,128)S(1)}, u32[]{:S(2)}, u32[]{:S(2)}) collective-permute-start(f32[640,128]{1,0:T(8,128)S(1)} %collective-permute-done.18.near), channel_id=1, source_target_pairs={{0,1},{1,0},{2,3},{3,2},{4,5},{5,4},{6,7},{7,6},{8,9},{9,8},{10,11... | collective-permute-start | bytes 983048 | tf_op jit(solution)/shard_map/ppermute | solution.py:17
  50.2 6.5 %collective-permute-start.41 = (f32[640,128]{1,0:T(8,128)S(1)}, f32[640,128]{1,0:T(8,128)S(1)}, u32[]{:S(2)}, u32[]{:S(2)}) collective-permute-start(f32[640,128]{1,0:T(8,128)S(1)} %collective-permute-done.20.opposite), channel_id=1, source_target_pairs={{0,1},{1,0},{2,3},{3,2},{4,5},{5,4},{6,7},{7,6},{8,9},{9,8},{10,11... | collective-permute-start | bytes 983048 | tf_op jit(solution)/shard_map/ppermute | solution.py:17
  50.7 6.6 %collective-permute-start.31 = (f32[640,128]{1,0:T(8,128)S(1)}, f32[640,128]{1,0:T(8,128)S(1)}, u32[]{:S(2)}, u32[]{:S(2)}) collective-permute-start(f32[640,128]{1,0:T(8,128)S(1)} %get-tuple-element.46.own), channel_id=1, source_target_pairs={{0,4},{1,13},{2,6},{3,15},{4,8},{5,1},{6,10},{7,3},{8,12},{9,5},{1... | collective-permute-start | bytes 983048 | tf_op jit(solution)/shard_map/ppermute | solution.py:29
  52.5 17.6 %collective-permute-start.38 = (f32[128,1280]{1,0:T(8,128)S(1)}, f32[128,1280]{1,0:T(8,128)S(1)}, u32[]{:S(2)}, u32[]{:S(2)}) collective-permute-start(f32[128,1280]{1,0:T(8,128)S(1)} %collective-permute-done.14.y), channel_id=1, source_target_pairs={{0,1},{1,0},{2,3},{3,2},{4,5},{5,4},{6,7},{7,6},{8,9},{9,8},{10,11... | collective-permute-start | bytes 1966088 | tf_op jit(solution)/shard_map/ppermute | solution.py:17
  52.5 1.0 %copy-start.2 = (f32[64,1280]{1,0:T(8,128)S(1)}, f32[64,1280]{1,0:T(8,128)}, u32[]{:S(2)}) copy-start(f32[64,1280]{1,0:T(8,128)} %own.7) | copy-start | bytes 983044
  55.1 11.8 %collective-permute-start.37 = (f32[32,1280]{1,0:T(8,128)S(1)}, f32[32,1280]{1,0:T(8,128)S(1)}, u32[]{:S(2)}, u32[]{:S(2)}) collective-permute-start(f32[32,1280]{1,0:T(8,128)S(1)} %collective-permute-done.13.far), channel_id=1, source_target_pairs={{0,1},{1,0},{2,3},{3,2},{4,5},{5,4},{6,7},{7,6},{8,9},{9,8},{10,11... | collective-permute-start | bytes 491528 | tf_op jit(solution)/shard_map/ppermute | solution.py:17
  55.6 11.8 %collective-permute-start.29 = (f32[640,128]{1,0:T(8,128)S(1)}, f32[640,128]{1,0:T(8,128)S(1)}, u32[]{:S(2)}, u32[]{:S(2)}) collective-permute-start(f32[640,128]{1,0:T(8,128)S(1)} %get-tuple-element.47.own2), channel_id=1, source_target_pairs={{0,4},{1,13},{2,6},{3,15},{4,8},{5,1},{6,10},{7,3},{8,12},{9,5},{1... | collective-permute-start | bytes 983048 | tf_op jit(solution)/shard_map/ppermute | solution.py:29
  56.7 10.1 %collective-permute-start.25 = (f32[480,128]{1,0:T(8,128)S(1)}, f32[480,128]{1,0:T(8,128)S(1)}, u32[]{:S(2)}, u32[]{:S(2)}) collective-permute-start(f32[480,128]{1,0:T(8,128)S(1)} %get-tuple-element.36.own), channel_id=1, source_target_pairs={{0,4},{1,13},{2,6},{3,15},{4,8},{5,1},{6,10},{7,3},{8,12},{9,5},{1... | collective-permute-start | bytes 737288 | tf_op jit(solution)/shard_map/ppermute | solution.py:29
  57.3 11.5 %collective-permute-start.32 = (f32[640,128]{1,0:T(8,128)S(1)}, f32[640,128]{1,0:T(8,128)S(1)}, u32[]{:S(2)}, u32[]{:S(2)}) collective-permute-start(f32[640,128]{1,0:T(8,128)S(1)} %collective-permute-done.31.near), channel_id=1, source_target_pairs={{0,4},{1,13},{2,6},{3,15},{4,8},{5,1},{6,10},{7,3},{8,12},{9,5},{1... | collective-permute-start | bytes 983048 | tf_op jit(solution)/shard_map/ppermute | solution.py:29
  66.8 11.6 %collective-permute-start.23 = (f32[480,128]{1,0:T(8,128)S(1)}, f32[480,128]{1,0:T(8,128)S(1)}, u32[]{:S(2)}, u32[]{:S(2)}) collective-permute-start(f32[480,128]{1,0:T(8,128)S(1)} %get-tuple-element.37.own2), channel_id=1, source_target_pairs={{0,4},{1,13},{2,6},{3,15},{4,8},{5,1},{6,10},{7,3},{8,12},{9,5},{1... | collective-permute-start | bytes 737288 | tf_op jit(solution)/shard_map/ppermute | solution.py:29
  66.8 12.1 %collective-permute-start.26 = (f32[480,128]{1,0:T(8,128)S(1)}, f32[480,128]{1,0:T(8,128)S(1)}, u32[]{:S(2)}, u32[]{:S(2)}) collective-permute-start(f32[480,128]{1,0:T(8,128)S(1)} %collective-permute-done.25.near), channel_id=1, source_target_pairs={{0,4},{1,13},{2,6},{3,15},{4,8},{5,1},{6,10},{7,3},{8,12},{9,5},{1... | collective-permute-start | bytes 737288 | tf_op jit(solution)/shard_map/ppermute | solution.py:29
  67.4 12.0 %collective-permute-start.33 = (f32[640,128]{1,0:T(8,128)S(1)}, f32[640,128]{1,0:T(8,128)S(1)}, u32[]{:S(2)}, u32[]{:S(2)}) collective-permute-start(f32[640,128]{1,0:T(8,128)S(1)} %collective-permute-done.31.near), channel_id=1, source_target_pairs={{0,1},{1,0},{2,3},{3,2},{4,5},{5,4},{6,7},{7,6},{8,9},{9,8},{10,11... | collective-permute-start | bytes 983048 | tf_op jit(solution)/shard_map/ppermute | solution.py:17
  68.8 10.1 %collective-permute-start.30 = (f32[640,128]{1,0:T(8,128)S(1)}, f32[640,128]{1,0:T(8,128)S(1)}, u32[]{:S(2)}, u32[]{:S(2)}) collective-permute-start(f32[640,128]{1,0:T(8,128)S(1)} %collective-permute-done.29.near2), channel_id=1, source_target_pairs={{0,1},{1,0},{2,3},{3,2},{4,5},{5,4},{6,7},{7,6},{8,9},{9,8},{10,11... | collective-permute-start | bytes 983048 | tf_op jit(solution)/shard_map/ppermute | solution.py:17
  70.2 9.2 %collective-permute-start.34 = (f32[640,128]{1,0:T(8,128)S(1)}, f32[640,128]{1,0:T(8,128)S(1)}, u32[]{:S(2)}, u32[]{:S(2)}) collective-permute-start(f32[640,128]{1,0:T(8,128)S(1)} %collective-permute-done.32.opposite), channel_id=1, source_target_pairs={{0,1},{1,0},{2,3},{3,2},{4,5},{5,4},{6,7},{7,6},{8,9},{9,8},{10,11... | collective-permute-start | bytes 983048 | tf_op jit(solution)/shard_map/ppermute | solution.py:17
  78.4 8.2 %collective-permute-start.27 = (f32[480,128]{1,0:T(8,128)S(1)}, f32[480,128]{1,0:T(8,128)S(1)}, u32[]{:S(2)}, u32[]{:S(2)}) collective-permute-start(f32[480,128]{1,0:T(8,128)S(1)} %collective-permute-done.25.near), channel_id=1, source_target_pairs={{0,1},{1,0},{2,3},{3,2},{4,5},{5,4},{6,7},{7,6},{8,9},{9,8},{10,11... | collective-permute-start | bytes 737288 | tf_op jit(solution)/shard_map/ppermute | solution.py:17
  78.9 7.7 %collective-permute-start.24 = (f32[480,128]{1,0:T(8,128)S(1)}, f32[480,128]{1,0:T(8,128)S(1)}, u32[]{:S(2)}, u32[]{:S(2)}) collective-permute-start(f32[480,128]{1,0:T(8,128)S(1)} %collective-permute-done.23.near2), channel_id=1, source_target_pairs={{0,1},{1,0},{2,3},{3,2},{4,5},{5,4},{6,7},{7,6},{8,9},{9,8},{10,11... | collective-permute-start | bytes 737288 | tf_op jit(solution)/shard_map/ppermute | solution.py:17
  79.0 7.6 %collective-permute-start.28 = (f32[480,128]{1,0:T(8,128)S(1)}, f32[480,128]{1,0:T(8,128)S(1)}, u32[]{:S(2)}, u32[]{:S(2)}) collective-permute-start(f32[480,128]{1,0:T(8,128)S(1)} %collective-permute-done.26.opposite), channel_id=1, source_target_pairs={{0,1},{1,0},{2,3},{3,2},{4,5},{5,4},{6,7},{7,6},{8,9},{9,8},{10,11... | collective-permute-start | bytes 737288 | tf_op jit(solution)/shard_map/ppermute | solution.py:17

commit v2 on v1

--- a/solution.py
+++ b/solution.py
@@ -130,22 +130,15 @@
         run((own2, far2, opposite2, near2))
 
 
-def cut_kernel(own, other, right, left_, far, right_o, left_o, far_o, y, y_o, amps, *rest):
+def cut_kernel(mine, others, y_mine, y_others, amps, *rest):
     out, rows, left = rest[-3:]
     col = lax.axis_index("col")
     y_hi, core = col // 2 % 2, col % 2
-
-    def put(value, slot, y_side, c):
-        rows[pl.ds(pl.multiple_of(slot * 128 + y_side * 64 + c * 32, 32), 32), :] = value
-
-    from_left = jnp.where(core == 0, 3, 1)
-    from_right = jnp.where(core == 0, 1, 3)
-    for c, parts in ((core, (own, right, left_, far)), (1 - core, (other, right_o, left_o, far_o))):
-        for part, slot in zip(parts, (0, from_left, from_right, 2)):
-            put(part[...], slot, y_hi, c)
-    for c, part in ((core, y), (1 - core, y_o)):
-        for k, slot in enumerate((0, from_left, from_right, 2)):
-            put(part[k * 32 : k * 32 + 32], slot, 1 - y_hi, c)
+    slots = (0, jnp.where(core == 0, 3, 1), jnp.where(core == 0, 1, 3), 2)
+    for y_side, c, part in ((y_hi, core, mine), (y_hi, 1 - core, others), (1 - y_hi, core, y_mine), (1 - y_hi, 1 - core, y_others)):
+        for k, slot in enumerate(slots):
+            at = pl.multiple_of(slot * 128 + y_side * 64 + c * 32, 32)
+            rows[pl.ds(at, 32), :] = part[k * 32 : k * 32 + 32]
     high, low = split(rows[...].T)
     left[:, :512] = high
     left[:, 512:1024] = low
@@ -216,7 +209,8 @@
     v_cut, v0, rest = v[:, :WIDE], v[:, WIDE : 2 * WIDE], v[:, 2 * WIDE :]
     y0, y1 = swap_y_hi(v0), swap_y_hi(rest)
     cut = [send_x(v_cut, 1), send_x(v_cut, -1), send_x(v_cut, 2)]
-    y_cut = swap_y_hi(jnp.concatenate([v_cut, *cut], 0))
+    cut = jnp.concatenate([v_cut, *cut], 0)
+    y_cut = swap_y_hi(cut)
     t0 = turn(WIDE, 1280, v, other, y0, swap_core(y0), 0)
     y1_other = swap_core(y1)
     t1, t2 = [turn(s, w, v, other, y1, y1_other, s - 2 * WIDE) for s, w, _ in CHUNKS[1:]]
@@ -234,8 +228,7 @@
     out = None
     for j, (start, width, tile) in enumerate(CHUNKS):
         if j == CUT_AT:
-            cut_other = [swap_core(p) for p in cut]
-            out = product_cut((v, other, *cut, *cut_other, y_cut, swap_core(y_cut)), amps, shape, out)
+            out = product_cut((cut, swap_core(cut), y_cut, swap_core(y_cut)), amps, shape, out)
         (f, s), (near_f, near_s), o = work[j]
         pieces = (f, swap_core(near_s), o, near_f, s, swap_core(near_f), swap_core(o), near_s)
         out = product(start, width, tile, pieces, amps, shape, out)

time: 92.7 us -> 91.9 us (level)
  starting transfers between devices: 47.8 us -> 46.3 us
  waiting for transfers between devices: 9.63 us -> 10.6 us
    ppermute x20 -> x18, starting transfers between devices: 12.3 us -> 11.2 us  [swap_core(): return lax.ppermute(v, 'col', [(i, i ^ 1) for i in range(16)])]
    ppermute x9, waiting for transfers between devices: 2.74 us -> 3.77 us  [shift_x(): lax.ppermute(v, 'col', [(i, (i + (4 if i % 2 == 0 else 12)) % 16) for i i...]
    ppermute x20 -> x18, waiting for transfers between devices: 3.31 us -> 3.3 us  [swap_core(): return lax.ppermute(v, 'col', [(i, i ^ 1) for i in range(16)])]
    unnamed x6 -> x4, local copies, waits for them, and re-layouts: 2.05 us -> 2.05 us
  transfers between devices with their start and end apart: 42 -> 40, of which waited for: 7 -> 8; matrix products, arithmetic and copies ran while one was open for 1% -> 1% of each run, Pallas kernels for 27% -> 27%
where the time goes in v2:
time: 91.9 us; the launch traced here: 91.7 us
  starting transfers between devices  46.3 us (50%)
  Pallas kernels  30.6 us (33%)
  waiting for transfers between devices  10.6 us (12%)
  local copies, waits for them, and re-layouts  4.04 us (4%)
    pallas_call x3, Pallas kernels, product(): pl.pallas_call(product_kernel, grid=(steps,), out_shape=jax.ShapeDtypeStr...  20.2 us
    ppermute x6, starting transfers between devices, shift_z(): return lax.ppermute(v, ('row', 'col'), pairs)  14.1 us
    ppermute x9, starting transfers between devices, shift_x(): lax.ppermute(v, 'col', [(i, (i + (4 if i % 2 == 0 else 12)) % 16) for i i...  12.3 us
    ppermute x18, starting transfers between devices, swap_core(): return lax.ppermute(v, 'col', [(i, i ^ 1) for i in range(16)])  11.2 us
    pallas_call x1, Pallas kernels, product_cut(): pl.pallas_call(cut_kernel, grid=(WIDE // 256,), out_shape=jax.ShapeDtypeS...  8.04 us
    ppermute x3, starting transfers between devices, send_x(): return lax.ppermute(v, 'col', [(i, (i + 4 * d) % 16) for i in range(16)])  4.28 us
    ppermute x3, starting transfers between devices, swap_y_hi(): return lax.ppermute(v, 'col', [(i, i ^ 2) for i in range(16)])  3.93 us
    ppermute x9, waiting for transfers between devices, shift_x(): lax.ppermute(v, 'col', [(i, (i + (4 if i % 2 == 0 else 12)) % 16) for i i...  3.77 us
  transfers between devices with their start and end apart: 40, of which 8 were waited for; matrix products, arithmetic and copies ran while one was open for 1% of the time, Pallas kernels for 27%

profile of v2, /device:TPU:1, one launch (start us, length us, event | category | flops | bytes accessed | tf_op | source)
XLA Modules:
  0.0 91.7 jit_solution(12973441558092895971)
XLA Ops:
  0.0 1.0 %slice.11 = f32[32,2240]{1,0:T(8,128)S(1)} slice(f32[32,4800]{1,0:T(8,128)} %own.5), slice={[0:32], [2560:4800]} | slice | bytes 573440 | tf_op jit(solution)/shard_map/slice | solution.py:209
  1.0 3.8 %collective-permute-start.21 = (f32[32,2240]{1,0:T(8,128)S(1)}, f32[32,2240]{1,0:T(8,128)S(1)}, u32[]{:S(2)}, u32[]{:S(2)}) collective-permute-start(f32[32,2240]{1,0:T(8,128)S(1)} %slice.11), channel_id=1, source_target_pairs={{0,2},{1,3},{2,0},{3,1},{4,6},{5,7},{6,4},{7,5},{8,10},{9,11},{10,... | collective-permute-start | bytes 860168 | tf_op jit(solution)/shard_map/ppermute | solution.py:21
  4.8 1.0 %fusion = (f32[32,1280]{1,0:T(8,128)S(1)}, f32[32,1280]{1,0:T(8,128)S(1)}) fusion(f32[32,4800]{1,0:T(8,128)} %own.5), kind=kLoop, calls=%fused_computation.1 | loop fusion | bytes 655360 | tf_op jit(solution)/shard_map/slice | solution.py:209
  5.8 1.3 %collective-permute-start.11 = (f32[32,1280]{1,0:T(8,128)S(1)}, f32[32,1280]{1,0:T(8,128)S(1)}, u32[]{:S(2)}, u32[]{:S(2)}) collective-permute-start(f32[32,1280]{1,0:T(8,128)S(1)} %get-tuple-element.52), channel_id=1, source_target_pairs={{0,4},{1,5},{2,6},{3,7},{4,8},{5,9},{6,10},{7,11},{8,12},{9,13},{1... | collective-permute-start | bytes 491528 | tf_op jit(solution)/shard_map/ppermute | solution.py:33
  7.1 1.5 %collective-permute-start.12 = (f32[32,1280]{1,0:T(8,128)S(1)}, f32[32,1280]{1,0:T(8,128)S(1)}, u32[]{:S(2)}, u32[]{:S(2)}) collective-permute-start(f32[32,1280]{1,0:T(8,128)S(1)} %get-tuple-element.52), channel_id=1, source_target_pairs={{0,12},{1,13},{2,14},{3,15},{4,0},{5,1},{6,2},{7,3},{8,4},{9,5},{1... | collective-permute-start | bytes 491528 | tf_op jit(solution)/shard_map/ppermute | solution.py:33
  8.6 1.5 %collective-permute-start.13 = (f32[32,1280]{1,0:T(8,128)S(1)}, f32[32,1280]{1,0:T(8,128)S(1)}, u32[]{:S(2)}, u32[]{:S(2)}) collective-permute-start(f32[32,1280]{1,0:T(8,128)S(1)} %get-tuple-element.52), channel_id=1, source_target_pairs={{0,8},{1,9},{2,10},{3,11},{4,12},{5,13},{6,14},{7,15},{8,0},{9,1},... | collective-permute-start | bytes 491528 | tf_op jit(solution)/shard_map/ppermute | solution.py:33
  10.1 0.1 collective-permute-start.16
  10.2 1.7 %collective-permute-done.11 = f32[32,1280]{1,0:T(8,128)S(1)} collective-permute-done((f32[32,1280]{1,0:T(8,128)S(1)}, f32[32,1280]{1,0:T(8,128)S(1)}, u32[]{:S(2)}, u32[]{:S(2)}) %collective-permute-start.11) | collective-permute-done | bytes 163872 | tf_op jit(solution)/shard_map/ppermute | solution.py:33
  11.9 0.4 collective-permute-start.5
  12.3 3.8 %collective-permute-start = (f32[64,1280]{1,0:T(8,128)}, f32[64,1280]{1,0:T(8,128)S(1)}, u32[]{:S(2)}, u32[]{:S(2)}) collective-permute-start(f32[64,1280]{1,0:T(8,128)} %own.6), channel_id=1, source_target_pairs={{0,16},{1,49},{2,18},{3,51},{4,20},{5,53},{6,22},{7,55},{8,24},{9,... | collective-permute-start | bytes 983048 | tf_op jit(solution)/shard_map/ppermute | solution.py:42
  16.0 0.3 collective-permute-done.13
  16.4 2.1 %collective-permute-start.1 = (f32[64,1280]{1,0:T(8,128)}, f32[64,1280]{1,0:T(8,128)S(1)}, u32[]{:S(2)}, u32[]{:S(2)}) collective-permute-start(f32[64,1280]{1,0:T(8,128)} %own.6), channel_id=1, source_target_pairs={{0,1},{1,0},{2,3},{3,2},{4,5},{5,4},{6,7},{7,6},{8,9},{9,8},{10,11... | collective-permute-start | bytes 983048 | tf_op jit(solution)/shard_map/ppermute | solution.py:17
  18.5 2.1 %collective-permute-start.15 = (f32[32,4800]{1,0:T(8,128)}, f32[32,4800]{1,0:T(8,128)S(1)}, u32[]{:S(2)}, u32[]{:S(2)}) collective-permute-start(f32[32,4800]{1,0:T(8,128)} %own.5), channel_id=1, source_target_pairs={{0,1},{1,0},{2,3},{3,2},{4,5},{5,4},{6,7},{7,6},{8,9},{9,8},{10,11... | collective-permute-start | bytes 1843208 | tf_op jit(solution)/shard_map/ppermute | solution.py:17
  20.6 0.0 collective-permute-start.17
  20.6 1.7 %collective-permute-done.17.y_other = f32[32,1280]{1,0:T(8,128)S(1)} collective-permute-done((f32[32,1280]{1,0:T(8,128)S(1)}, f32[32,1280]{1,0:T(8,128)S(1)}, u32[]{:S(2)}, u32[]{:S(2)}) %collective-permute-start.17) | collective-permute-done | bytes 163872 | tf_op jit(solution)/shard_map/ppermute | solution.py:17
  22.3 0.1 collective-permute-start.14
  22.4 0.0 collective-permute-done.5.y_own
  22.4 3.8 %collective-permute-start.6 = (f32[64,1280]{1,0:T(8,128)S(1)}, f32[64,1280]{1,0:T(8,128)S(1)}, u32[]{:S(2)}, u32[]{:S(2)}) collective-permute-start(f32[64,1280]{1,0:T(8,128)S(1)} %collective-permute-done.5.y_own), channel_id=1, source_target_pairs={{0,16},{1,49},{2,18},{3,51},{4,20},{5,53},{6,22},{7,55},{8,24},{9,... | collective-permute-start | bytes 983048 | tf_op jit(solution)/shard_map/ppermute | solution.py:42
  26.2 0.5 collective-permute-start.22
  26.7 1.5 %collective-permute-done.22.y_other = f32[32,2240]{1,0:T(8,128)S(1)} collective-permute-done((f32[32,2240]{1,0:T(8,128)S(1)}, f32[32,2240]{1,0:T(8,128)S(1)}, u32[]{:S(2)}, u32[]{:S(2)}) %collective-permute-start.22) | collective-permute-done | bytes 286752 | tf_op jit(solution)/shard_map/ppermute | solution.py:17
  28.2 1.2 %collective-permute-start.4 = (f32[64,1280]{1,0:T(8,128)S(1)}, f32[64,1280]{1,0:T(8,128)S(1)}, u32[]{:S(2)}, u32[]{:S(2)}) collective-permute-start(f32[64,1280]{1,0:T(8,128)S(1)} %collective-permute-done.near), channel_id=1, source_target_pairs={{0,16},{1,49},{2,18},{3,51},{4,20},{5,53},{6,22},{7,55},{8,24},{9,... | collective-permute-start | bytes 983048 | tf_op jit(solution)/shard_map/ppermute | solution.py:42
  29.4 1.7 %collective-permute-start.2 = (f32[64,1280]{1,0:T(8,128)S(1)}, f32[64,1280]{1,0:T(8,128)S(1)}, u32[]{:S(2)}, u32[]{:S(2)}) collective-permute-start(f32[64,1280]{1,0:T(8,128)S(1)} %collective-permute-done.1), channel_id=1, source_target_pairs={{0,16},{1,49},{2,18},{3,51},{4,20},{5,53},{6,22},{7,55},{8,24},{9,... | collective-permute-start | bytes 983048 | tf_op jit(solution)/shard_map/ppermute | solution.py:42
  31.1 1.1 %copy-done = f32[32,4800]{1,0:T(8,128)S(1)} copy-done((f32[32,4800]{1,0:T(8,128)S(1)}, f32[32,4800]{1,0:T(8,128)}, u32[]{:S(2)}) %copy-start) | copy-done | bytes 614424
  32.2 0.3 shard_map.28
  32.5 2.3 %collective-permute-start.18 = (f32[640,128]{1,0:T(8,128)S(1)}, f32[640,128]{1,0:T(8,128)S(1)}, u32[]{:S(2)}, u32[]{:S(2)}) collective-permute-start(f32[640,128]{1,0:T(8,128)S(1)} %get-tuple-element.28.own), channel_id=1, source_target_pairs={{0,4},{1,13},{2,6},{3,15},{4,8},{5,1},{6,10},{7,3},{8,12},{9,5},{1... | collective-permute-start | bytes 983048 | tf_op jit(solution)/shard_map/ppermute | solution.py:29
  34.8 0.0 collective-permute-done.7
  34.8 1.0 %collective-permute-start.8 = (f32[64,1280]{1,0:T(8,128)S(1)}, f32[64,1280]{1,0:T(8,128)S(1)}, u32[]{:S(2)}, u32[]{:S(2)}) collective-permute-start(f32[64,1280]{1,0:T(8,128)S(1)} %collective-permute-done.7), channel_id=1, source_target_pairs={{0,16},{1,49},{2,18},{3,51},{4,20},{5,53},{6,22},{7,55},{8,24},{9,... | collective-permute-start | bytes 983048 | tf_op jit(solution)/shard_map/ppermute | solution.py:42
  35.8 0.0 collective-permute-done.4.opposite
  35.9 1.3 %collective-permute-start.19 = (f32[640,128]{1,0:T(8,128)S(1)}, f32[640,128]{1,0:T(8,128)S(1)}, u32[]{:S(2)}, u32[]{:S(2)}) collective-permute-start(f32[640,128]{1,0:T(8,128)S(1)} %get-tuple-element.29.own2), channel_id=1, source_target_pairs={{0,4},{1,13},{2,6},{3,15},{4,8},{5,1},{6,10},{7,3},{8,12},{9,5},{1... | collective-permute-start | bytes 983048 | tf_op jit(solution)/shard_map/ppermute | solution.py:29
  37.1 0.8 collective-permute-done.2
  37.9 2.7 %collective-permute-start.10 = (f32[64,1280]{1,0:T(8,128)S(1)}, f32[64,1280]{1,0:T(8,128)S(1)}, u32[]{:S(2)}, u32[]{:S(2)}) collective-permute-start(f32[64,1280]{1,0:T(8,128)S(1)} %collective-permute-done.6.y_near), channel_id=1, source_target_pairs={{0,16},{1,49},{2,18},{3,51},{4,20},{5,53},{6,22},{7,55},{8,24},{9,... | collective-permute-start | bytes 983048 | tf_op jit(solution)/shard_map/ppermute | solution.py:42
  40.6 0.4 collective-permute-start.3
  41.0 0.0 collective-permute-done.18.near
  41.0 2.7 %collective-permute-start.20 = (f32[640,128]{1,0:T(8,128)S(1)}, f32[640,128]{1,0:T(8,128)S(1)}, u32[]{:S(2)}, u32[]{:S(2)}) collective-permute-start(f32[640,128]{1,0:T(8,128)S(1)} %collective-permute-done.18.near), channel_id=1, source_target_pairs={{0,4},{1,13},{2,6},{3,15},{4,8},{5,1},{6,10},{7,3},{8,12},{9,5},{1... | collective-permute-start | bytes 983048 | tf_op jit(solution)/shard_map/ppermute | solution.py:29
  43.7 0.0 collective-permute-done.8
  43.7 0.0 collective-permute-start.9
  43.7 0.3 shard_map.29
  44.0 0.3 shard_map.30
  44.2 0.7 collective-permute-done.10.y_opposite
  45.0 0.0 collective-permute-done.3.far
  45.0 2.7 %collective-permute-done.20.opposite = f32[640,128]{1,0:T(8,128)S(1)} collective-permute-done((f32[640,128]{1,0:T(8,128)S(1)}, f32[640,128]{1,0:T(8,128)S(1)}, u32[]{:S(2)}, u32[]{:S(2)}) %collective-permute-start.20) | collective-permute-done | bytes 327712 | tf_op jit(solution)/shard_map/ppermute | solution.py:29
  47.7 1.9 %collective-permute-start.37 = (f32[640,128]{1,0:T(8,128)S(1)}, f32[640,128]{1,0:T(8,128)S(1)}, u32[]{:S(2)}, u32[]{:S(2)}) collective-permute-start(f32[640,128]{1,0:T(8,128)S(1)} %collective-permute-done.19.near2), channel_id=1, source_target_pairs={{0,1},{1,0},{2,3},{3,2},{4,5},{5,4},{6,7},{7,6},{8,9},{9,8},{10,11... | collective-permute-start | bytes 983048 | tf_op jit(solution)/shard_map/ppermute | solution.py:17
  49.6 0.0 collective-permute-start.38
  49.6 0.5 collective-permute-start.39
  50.1 1.8 %collective-permute-start.31 = (f32[640,128]{1,0:T(8,128)S(1)}, f32[640,128]{1,0:T(8,128)S(1)}, u32[]{:S(2)}, u32[]{:S(2)}) collective-permute-start(f32[640,128]{1,0:T(8,128)S(1)} %get-tuple-element.44.own), channel_id=1, source_target_pairs={{0,4},{1,13},{2,6},{3,15},{4,8},{5,1},{6,10},{7,3},{8,12},{9,5},{1... | collective-permute-start | bytes 983048 | tf_op jit(solution)/shard_map/ppermute | solution.py:29
  52.0 0.5 collective-permute-start.36
  52.5 1.0 %copy-done.1 = f32[64,1280]{1,0:T(8,128)S(1)} copy-done((f32[64,1280]{1,0:T(8,128)S(1)}, f32[64,1280]{1,0:T(8,128)}, u32[]{:S(2)}) %copy-start.1) | copy-done | bytes 327704
  53.4 1.5 %shard_map.31.amps = bf16[1536,1280]{1,0:T(8,128)(2,1)S(1)} custom-call(f32[64,1280]{1,0:T(8,128)S(1)} %copy-done.1, f32[64,1280]{1,0:T(8,128)S(1)} %collective-permute-done.near, f32[64,1280]{1,0:T(8,128)S(1)} %collective-permute-done.3.far, f32[64,1280]{1,0:T(8,128)S(1)} %collective-permute-done.4.opposite, f32[64,1280]{1,0:T(8,128)S(1)} %collective-permute-done.5.y_own, ...), custom_call_target="tpu_custom_call" | custom-call | flops 3145728 | bytes 6291456 | tf_op jit(solution)/shard_map/pallas_call | solution.py:72
  55.0 0.7 collective-permute-start.29
  55.7 0.7 collective-permute-start.25
  56.4 2.7 %collective-permute-start.32 = (f32[640,128]{1,0:T(8,128)S(1)}, f32[640,128]{1,0:T(8,128)S(1)}, u32[]{:S(2)}, u32[]{:S(2)}) collective-permute-start(f32[640,128]{1,0:T(8,128)S(1)} %collective-permute-done.31.near), channel_id=1, source_target_pairs={{0,4},{1,13},{2,6},{3,15},{4,8},{5,1},{6,10},{7,3},{8,12},{9,5},{1... | collective-permute-start | bytes 983048 | tf_op jit(solution)/shard_map/ppermute | solution.py:29
  59.1 7.1 %shard_map.32.rest_0_ = f32[4800,1280]{1,0:T(8,128)} custom-call(f32[640,128]{1,0:T(8,128)S(1)} %get-tuple-element.28.own, f32[640,128]{1,0:T(8,128)S(1)} %collective-permute-done.37.far, f32[640,128]{1,0:T(8,128)S(1)} %collective-permute-done.20.opposite, f32[640,128]{1,0:T(8,128)S(1)} %collective-permute-done.18.near, ...), custom_call_target="tpu_custom_call" | custom-call | flops 5033164800 | bytes 6553600 | tf_op jit(solution)/shard_map/pallas_call | solution.py:187
  66.2 0.0 collective-permute-start.23
  66.2 0.1 collective-permute-start.26
  66.4 1.0 %collective-permute-done.32.opposite = f32[640,128]{1,0:T(8,128)S(1)} collective-permute-done((f32[640,128]{1,0:T(8,128)S(1)}, f32[640,128]{1,0:T(8,128)S(1)}, u32[]{:S(2)}, u32[]{:S(2)}) %collective-permute-start.32) | collective-permute-done | bytes 327712 | tf_op jit(solution)/shard_map/ppermute | solution.py:29
  67.4 2.1 %collective-permute-start.33 = (f32[640,128]{1,0:T(8,128)S(1)}, f32[640,128]{1,0:T(8,128)S(1)}, u32[]{:S(2)}, u32[]{:S(2)}) collective-permute-start(f32[640,128]{1,0:T(8,128)S(1)} %collective-permute-done.31.near), channel_id=1, source_target_pairs={{0,1},{1,0},{2,3},{3,2},{4,5},{5,4},{6,7},{7,6},{8,9},{9,8},{10,11... | collective-permute-start | bytes 983048 | tf_op jit(solution)/shard_map/ppermute | solution.py:17
  69.5 0.0 collective-permute-start.30
  69.5 0.5 collective-permute-start.34
  70.0 8.0 %shard_map.33.rest_0_ = f32[4800,1280]{1,0:T(8,128)} custom-call(f32[128,1280]{1,0:T(8,128)S(1)} %pad_maximum_fusion.mine, f32[128,1280]{1,0:T(8,128)S(1)} %collective-permute-done.35.others, f32[128,1280]{1,0:T(8,128)S(1)} %collective-permute-done.14.y_mine, f32[128,1280]{1,0:T(8,128)S(1)} %collective-permute-done.36.y_others, ...), custom_call_target="tpu_custom_call", output_to_operand_aliasing={{}: (5, {})} | custom-call | flops 5033164800 | bytes 6553600 | tf_op jit(solution)/shard_map/pallas_call | solution.py:158
  78.0 0.1 collective-permute-start.27
  78.1 0.4 collective-permute-start.24
  78.6 0.1 collective-permute-start.28
  78.7 7.2 %shard_map.34.rest_0_ = f32[4800,1280]{1,0:T(8,128)} custom-call(f32[640,128]{1,0:T(8,128)S(1)} %get-tuple-element.44.own, f32[640,128]{1,0:T(8,128)S(1)} %collective-permute-done.30.far, f32[640,128]{1,0:T(8,128)S(1)} %collective-permute-done.32.opposite, f32[640,128]{1,0:T(8,128)S(1)} %collective-permute-done.31.near, ...), custom_call_target="tpu_custom_call", output_to_operand_aliasing={{}: (9, {})} | custom-call | flops 5033164800 | bytes 6553600 | tf_op jit(solution)/shard_map/pallas_call | solution.py:187
  85.9 5.9 %shard_map.35 = f32[4800,1280]{1,0:T(8,128)} custom-call(f32[480,128]{1,0:T(8,128)S(1)} %get-tuple-element.34.own, f32[480,128]{1,0:T(8,128)S(1)} %collective-permute-done.24.far, f32[480,128]{1,0:T(8,128)S(1)} %collective-permute-done.26.opposite, f32[480,128]{1,0:T(8,128)S(1)} %collective-permute-done.25.near, ...), custom_call_target="tpu_custom_call", output_to_operand_aliasing={{}: (9, {})} | custom-call | flops 3774873600 | bytes 4915200 | tf_op jit(solution)/shard_map/pallas_call | solution.py:187
  (31 shorter events, 0.1 us)
Async XLA Ops:
  1.0 19.6 %collective-permute-start.21 = (f32[32,2240]{1,0:T(8,128)S(1)}, f32[32,2240]{1,0:T(8,128)S(1)}, u32[]{:S(2)}, u32[]{:S(2)}) collective-permute-start(f32[32,2240]{1,0:T(8,128)S(1)} %slice.11), channel_id=1, source_target_pairs={{0,2},{1,3},{2,0},{3,1},{4,6},{5,7},{6,4},{7,5},{8,10},{9,11},{10,... | collective-permute-start | bytes 860168 | tf_op jit(solution)/shard_map/ppermute | solution.py:21
  5.8 6.0 %collective-permute-start.11 = (f32[32,1280]{1,0:T(8,128)S(1)}, f32[32,1280]{1,0:T(8,128)S(1)}, u32[]{:S(2)}, u32[]{:S(2)}) collective-permute-start(f32[32,1280]{1,0:T(8,128)S(1)} %get-tuple-element.52), channel_id=1, source_target_pairs={{0,4},{1,5},{2,6},{3,7},{4,8},{5,9},{6,10},{7,11},{8,12},{9,13},{1... | collective-permute-start | bytes 491528 | tf_op jit(solution)/shard_map/ppermute | solution.py:33
  7.1 5.1 %collective-permute-start.12 = (f32[32,1280]{1,0:T(8,128)S(1)}, f32[32,1280]{1,0:T(8,128)S(1)}, u32[]{:S(2)}, u32[]{:S(2)}) collective-permute-start(f32[32,1280]{1,0:T(8,128)S(1)} %get-tuple-element.52), channel_id=1, source_target_pairs={{0,12},{1,13},{2,14},{3,15},{4,0},{5,1},{6,2},{7,3},{8,4},{9,5},{1... | collective-permute-start | bytes 491528 | tf_op jit(solution)/shard_map/ppermute | solution.py:33
  8.6 7.8 %collective-permute-start.13 = (f32[32,1280]{1,0:T(8,128)S(1)}, f32[32,1280]{1,0:T(8,128)S(1)}, u32[]{:S(2)}, u32[]{:S(2)}) collective-permute-start(f32[32,1280]{1,0:T(8,128)S(1)} %get-tuple-element.52), channel_id=1, source_target_pairs={{0,8},{1,9},{2,10},{3,11},{4,12},{5,13},{6,14},{7,15},{8,0},{9,1},... | collective-permute-start | bytes 491528 | tf_op jit(solution)/shard_map/ppermute | solution.py:33
  10.1 8.3 %collective-permute-start.16 = (f32[32,1280]{1,0:T(8,128)S(1)}, f32[32,1280]{1,0:T(8,128)S(1)}, u32[]{:S(2)}, u32[]{:S(2)}) collective-permute-start(f32[32,1280]{1,0:T(8,128)S(1)} %get-tuple-element.51), channel_id=1, source_target_pairs={{0,2},{1,3},{2,0},{3,1},{4,6},{5,7},{6,4},{7,5},{8,10},{9,11},{10,... | collective-permute-start | bytes 491528 | tf_op jit(solution)/shard_map/ppermute | solution.py:21
  11.9 10.5 %collective-permute-start.5 = (f32[64,1280]{1,0:T(8,128)}, f32[64,1280]{1,0:T(8,128)S(1)}, u32[]{:S(2)}, u32[]{:S(2)}) collective-permute-start(f32[64,1280]{1,0:T(8,128)} %own.6), channel_id=1, source_target_pairs={{0,64},{16,80},{32,96},{48,112},{64,0},{80,16},{96,32},{112,48},{1... | collective-permute-start | bytes 983048 | tf_op jit(solution)/shard_map/ppermute | solution.py:25
  12.3 13.9 %collective-permute-start = (f32[64,1280]{1,0:T(8,128)}, f32[64,1280]{1,0:T(8,128)S(1)}, u32[]{:S(2)}, u32[]{:S(2)}) collective-permute-start(f32[64,1280]{1,0:T(8,128)} %own.6), channel_id=1, source_target_pairs={{0,16},{1,49},{2,18},{3,51},{4,20},{5,53},{6,22},{7,55},{8,24},{9,... | collective-permute-start | bytes 983048 | tf_op jit(solution)/shard_map/ppermute | solution.py:42
  16.4 9.8 %collective-permute-start.1 = (f32[64,1280]{1,0:T(8,128)}, f32[64,1280]{1,0:T(8,128)S(1)}, u32[]{:S(2)}, u32[]{:S(2)}) collective-permute-start(f32[64,1280]{1,0:T(8,128)} %own.6), channel_id=1, source_target_pairs={{0,1},{1,0},{2,3},{3,2},{4,5},{5,4},{6,7},{7,6},{8,9},{9,8},{10,11... | collective-permute-start | bytes 983048 | tf_op jit(solution)/shard_map/ppermute | solution.py:17
  18.5 10.9 %collective-permute-start.15 = (f32[32,4800]{1,0:T(8,128)}, f32[32,4800]{1,0:T(8,128)S(1)}, u32[]{:S(2)}, u32[]{:S(2)}) collective-permute-start(f32[32,4800]{1,0:T(8,128)} %own.5), channel_id=1, source_target_pairs={{0,1},{1,0},{2,3},{3,2},{4,5},{5,4},{6,7},{7,6},{8,9},{9,8},{10,11... | collective-permute-start | bytes 1843208 | tf_op jit(solution)/shard_map/ppermute | solution.py:17
  20.6 1.8 %collective-permute-start.17 = (f32[32,1280]{1,0:T(8,128)S(1)}, f32[32,1280]{1,0:T(8,128)S(1)}, u32[]{:S(2)}, u32[]{:S(2)}) collective-permute-start(f32[32,1280]{1,0:T(8,128)S(1)} %collective-permute-done.16.y_own), channel_id=1, source_target_pairs={{0,1},{1,0},{2,3},{3,2},{4,5},{5,4},{6,7},{7,6},{8,9},{9,8},{10,11... | collective-permute-start | bytes 491528 | tf_op jit(solution)/shard_map/ppermute | solution.py:17
  22.3 18.3 %collective-permute-start.14 = (f32[128,1280]{1,0:T(8,128)S(1)}, f32[128,1280]{1,0:T(8,128)S(1)}, u32[]{:S(2)}, u32[]{:S(2)}) collective-permute-start(f32[128,1280]{1,0:T(8,128)S(1)} %pad_maximum_fusion.mine), channel_id=1, source_target_pairs={{0,2},{1,3},{2,0},{3,1},{4,6},{5,7},{6,4},{7,5},{8,10},{9,11},{10,... | collective-permute-start | bytes 1966088 | tf_op jit(solution)/shard_map/ppermute | solution.py:21
  22.4 10.1 %collective-permute-start.6 = (f32[64,1280]{1,0:T(8,128)S(1)}, f32[64,1280]{1,0:T(8,128)S(1)}, u32[]{:S(2)}, u32[]{:S(2)}) collective-permute-start(f32[64,1280]{1,0:T(8,128)S(1)} %collective-permute-done.5.y_own), channel_id=1, source_target_pairs={{0,16},{1,49},{2,18},{3,51},{4,20},{5,53},{6,22},{7,55},{8,24},{9,... | collective-permute-start | bytes 983048 | tf_op jit(solution)/shard_map/ppermute | solution.py:42
  26.1 8.7 %collective-permute-start.7 = (f32[64,1280]{1,0:T(8,128)S(1)}, f32[64,1280]{1,0:T(8,128)S(1)}, u32[]{:S(2)}, u32[]{:S(2)}) collective-permute-start(f32[64,1280]{1,0:T(8,128)S(1)} %collective-permute-done.5.y_own), channel_id=1, source_target_pairs={{0,1},{1,0},{2,3},{3,2},{4,5},{5,4},{6,7},{7,6},{8,9},{9,8},{10,11... | collective-permute-start | bytes 983048 | tf_op jit(solution)/shard_map/ppermute | solution.py:17
  26.2 2.0 %collective-permute-start.22 = (f32[32,2240]{1,0:T(8,128)S(1)}, f32[32,2240]{1,0:T(8,128)S(1)}, u32[]{:S(2)}, u32[]{:S(2)}) collective-permute-start(f32[32,2240]{1,0:T(8,128)S(1)} %collective-permute-done.21.y_own), channel_id=1, source_target_pairs={{0,1},{1,0},{2,3},{3,2},{4,5},{5,4},{6,7},{7,6},{8,9},{9,8},{10,11... | collective-permute-start | bytes 860168 | tf_op jit(solution)/shard_map/ppermute | solution.py:17
  28.2 7.7 %collective-permute-start.4 = (f32[64,1280]{1,0:T(8,128)S(1)}, f32[64,1280]{1,0:T(8,128)S(1)}, u32[]{:S(2)}, u32[]{:S(2)}) collective-permute-start(f32[64,1280]{1,0:T(8,128)S(1)} %collective-permute-done.near), channel_id=1, source_target_pairs={{0,16},{1,49},{2,18},{3,51},{4,20},{5,53},{6,22},{7,55},{8,24},{9,... | collective-permute-start | bytes 983048 | tf_op jit(solution)/shard_map/ppermute | solution.py:42
  29.4 8.5 %collective-permute-start.2 = (f32[64,1280]{1,0:T(8,128)S(1)}, f32[64,1280]{1,0:T(8,128)S(1)}, u32[]{:S(2)}, u32[]{:S(2)}) collective-permute-start(f32[64,1280]{1,0:T(8,128)S(1)} %collective-permute-done.1), channel_id=1, source_target_pairs={{0,16},{1,49},{2,18},{3,51},{4,20},{5,53},{6,22},{7,55},{8,24},{9,... | collective-permute-start | bytes 983048 | tf_op jit(solution)/shard_map/ppermute | solution.py:42
  31.1 1.1 %copy-start = (f32[32,4800]{1,0:T(8,128)S(1)}, f32[32,4800]{1,0:T(8,128)}, u32[]{:S(2)}) copy-start(f32[32,4800]{1,0:T(8,128)} %own.5) | copy-start | bytes 1843204
  32.5 8.5 %collective-permute-start.18 = (f32[640,128]{1,0:T(8,128)S(1)}, f32[640,128]{1,0:T(8,128)S(1)}, u32[]{:S(2)}, u32[]{:S(2)}) collective-permute-start(f32[640,128]{1,0:T(8,128)S(1)} %get-tuple-element.28.own), channel_id=1, source_target_pairs={{0,4},{1,13},{2,6},{3,15},{4,8},{5,1},{6,10},{7,3},{8,12},{9,5},{1... | collective-permute-start | bytes 983048 | tf_op jit(solution)/shard_map/ppermute | solution.py:29
  34.8 8.8 %collective-permute-start.8 = (f32[64,1280]{1,0:T(8,128)S(1)}, f32[64,1280]{1,0:T(8,128)S(1)}, u32[]{:S(2)}, u32[]{:S(2)}) collective-permute-start(f32[64,1280]{1,0:T(8,128)S(1)} %collective-permute-done.7), channel_id=1, source_target_pairs={{0,16},{1,49},{2,18},{3,51},{4,20},{5,53},{6,22},{7,55},{8,24},{9,... | collective-permute-start | bytes 983048 | tf_op jit(solution)/shard_map/ppermute | solution.py:42
  35.9 8.4 %collective-permute-start.19 = (f32[640,128]{1,0:T(8,128)S(1)}, f32[640,128]{1,0:T(8,128)S(1)}, u32[]{:S(2)}, u32[]{:S(2)}) collective-permute-start(f32[640,128]{1,0:T(8,128)S(1)} %get-tuple-element.29.own2), channel_id=1, source_target_pairs={{0,4},{1,13},{2,6},{3,15},{4,8},{5,1},{6,10},{7,3},{8,12},{9,5},{1... | collective-permute-start | bytes 983048 | tf_op jit(solution)/shard_map/ppermute | solution.py:29
  37.9 7.0 %collective-permute-start.10 = (f32[64,1280]{1,0:T(8,128)S(1)}, f32[64,1280]{1,0:T(8,128)S(1)}, u32[]{:S(2)}, u32[]{:S(2)}) collective-permute-start(f32[64,1280]{1,0:T(8,128)S(1)} %collective-permute-done.6.y_near), channel_id=1, source_target_pairs={{0,16},{1,49},{2,18},{3,51},{4,20},{5,53},{6,22},{7,55},{8,24},{9,... | collective-permute-start | bytes 983048 | tf_op jit(solution)/shard_map/ppermute | solution.py:42
  40.6 4.4 %collective-permute-start.3 = (f32[64,1280]{1,0:T(8,128)S(1)}, f32[64,1280]{1,0:T(8,128)S(1)}, u32[]{:S(2)}, u32[]{:S(2)}) collective-permute-start(f32[64,1280]{1,0:T(8,128)S(1)} %collective-permute-done.2), channel_id=1, source_target_pairs={{0,1},{1,0},{2,3},{3,2},{4,5},{5,4},{6,7},{7,6},{8,9},{9,8},{10,11... | collective-permute-start | bytes 983048 | tf_op jit(solution)/shard_map/ppermute | solution.py:17
  41.0 6.7 %collective-permute-start.20 = (f32[640,128]{1,0:T(8,128)S(1)}, f32[640,128]{1,0:T(8,128)S(1)}, u32[]{:S(2)}, u32[]{:S(2)}) collective-permute-start(f32[640,128]{1,0:T(8,128)S(1)} %collective-permute-done.18.near), channel_id=1, source_target_pairs={{0,4},{1,13},{2,6},{3,15},{4,8},{5,1},{6,10},{7,3},{8,12},{9,5},{1... | collective-permute-start | bytes 983048 | tf_op jit(solution)/shard_map/ppermute | solution.py:29
  43.7 4.0 %collective-permute-start.9 = (f32[64,1280]{1,0:T(8,128)S(1)}, f32[64,1280]{1,0:T(8,128)S(1)}, u32[]{:S(2)}, u32[]{:S(2)}) collective-permute-start(f32[64,1280]{1,0:T(8,128)S(1)} %collective-permute-done.8), channel_id=1, source_target_pairs={{0,1},{1,0},{2,3},{3,2},{4,5},{5,4},{6,7},{7,6},{8,9},{9,8},{10,11... | collective-permute-start | bytes 983048 | tf_op jit(solution)/shard_map/ppermute | solution.py:17
  47.7 4.3 %collective-permute-start.37 = (f32[640,128]{1,0:T(8,128)S(1)}, f32[640,128]{1,0:T(8,128)S(1)}, u32[]{:S(2)}, u32[]{:S(2)}) collective-permute-start(f32[640,128]{1,0:T(8,128)S(1)} %collective-permute-done.19.near2), channel_id=1, source_target_pairs={{0,1},{1,0},{2,3},{3,2},{4,5},{5,4},{6,7},{7,6},{8,9},{9,8},{10,11... | collective-permute-start | bytes 983048 | tf_op jit(solution)/shard_map/ppermute | solution.py:17
  49.6 5.4 %collective-permute-start.38 = (f32[640,128]{1,0:T(8,128)S(1)}, f32[640,128]{1,0:T(8,128)S(1)}, u32[]{:S(2)}, u32[]{:S(2)}) collective-permute-start(f32[640,128]{1,0:T(8,128)S(1)} %collective-permute-done.18.near), channel_id=1, source_target_pairs={{0,1},{1,0},{2,3},{3,2},{4,5},{5,4},{6,7},{7,6},{8,9},{9,8},{10,11... | collective-permute-start | bytes 983048 | tf_op jit(solution)/shard_map/ppermute | solution.py:17
  49.6 6.1 %collective-permute-start.39 = (f32[640,128]{1,0:T(8,128)S(1)}, f32[640,128]{1,0:T(8,128)S(1)}, u32[]{:S(2)}, u32[]{:S(2)}) collective-permute-start(f32[640,128]{1,0:T(8,128)S(1)} %collective-permute-done.20.opposite), channel_id=1, source_target_pairs={{0,1},{1,0},{2,3},{3,2},{4,5},{5,4},{6,7},{7,6},{8,9},{9,8},{10,11... | collective-permute-start | bytes 983048 | tf_op jit(solution)/shard_map/ppermute | solution.py:17
  50.1 6.3 %collective-permute-start.31 = (f32[640,128]{1,0:T(8,128)S(1)}, f32[640,128]{1,0:T(8,128)S(1)}, u32[]{:S(2)}, u32[]{:S(2)}) collective-permute-start(f32[640,128]{1,0:T(8,128)S(1)} %get-tuple-element.44.own), channel_id=1, source_target_pairs={{0,4},{1,13},{2,6},{3,15},{4,8},{5,1},{6,10},{7,3},{8,12},{9,5},{1... | collective-permute-start | bytes 983048 | tf_op jit(solution)/shard_map/ppermute | solution.py:29
  51.9 17.5 %collective-permute-start.35 = (f32[128,1280]{1,0:T(8,128)S(1)}, f32[128,1280]{1,0:T(8,128)S(1)}, u32[]{:S(2)}, u32[]{:S(2)}) collective-permute-start(f32[128,1280]{1,0:T(8,128)S(1)} %pad_maximum_fusion.mine), channel_id=1, source_target_pairs={{0,1},{1,0},{2,3},{3,2},{4,5},{5,4},{6,7},{7,6},{8,9},{9,8},{10,11... | collective-permute-start | bytes 1966088 | tf_op jit(solution)/shard_map/ppermute | solution.py:17
  52.0 17.5 %collective-permute-start.36 = (f32[128,1280]{1,0:T(8,128)S(1)}, f32[128,1280]{1,0:T(8,128)S(1)}, u32[]{:S(2)}, u32[]{:S(2)}) collective-permute-start(f32[128,1280]{1,0:T(8,128)S(1)} %collective-permute-done.14.y_mine), channel_id=1, source_target_pairs={{0,1},{1,0},{2,3},{3,2},{4,5},{5,4},{6,7},{7,6},{8,9},{9,8},{10,11... | collective-permute-start | bytes 1966088 | tf_op jit(solution)/shard_map/ppermute | solution.py:17
  52.5 1.0 %copy-start.1 = (f32[64,1280]{1,0:T(8,128)S(1)}, f32[64,1280]{1,0:T(8,128)}, u32[]{:S(2)}) copy-start(f32[64,1280]{1,0:T(8,128)} %own.6) | copy-start | bytes 983044
  55.0 11.3 %collective-permute-start.29 = (f32[640,128]{1,0:T(8,128)S(1)}, f32[640,128]{1,0:T(8,128)S(1)}, u32[]{:S(2)}, u32[]{:S(2)}) collective-permute-start(f32[640,128]{1,0:T(8,128)S(1)} %get-tuple-element.45.own2), channel_id=1, source_target_pairs={{0,4},{1,13},{2,6},{3,15},{4,8},{5,1},{6,10},{7,3},{8,12},{9,5},{1... | collective-permute-start | bytes 983048 | tf_op jit(solution)/shard_map/ppermute | solution.py:29
  55.7 10.6 %collective-permute-start.25 = (f32[480,128]{1,0:T(8,128)S(1)}, f32[480,128]{1,0:T(8,128)S(1)}, u32[]{:S(2)}, u32[]{:S(2)}) collective-permute-start(f32[480,128]{1,0:T(8,128)S(1)} %get-tuple-element.34.own), channel_id=1, source_target_pairs={{0,4},{1,13},{2,6},{3,15},{4,8},{5,1},{6,10},{7,3},{8,12},{9,5},{1... | collective-permute-start | bytes 737288 | tf_op jit(solution)/shard_map/ppermute | solution.py:29
  56.4 11.0 %collective-permute-start.32 = (f32[640,128]{1,0:T(8,128)S(1)}, f32[640,128]{1,0:T(8,128)S(1)}, u32[]{:S(2)}, u32[]{:S(2)}) collective-permute-start(f32[640,128]{1,0:T(8,128)S(1)} %collective-permute-done.31.near), channel_id=1, source_target_pairs={{0,4},{1,13},{2,6},{3,15},{4,8},{5,1},{6,10},{7,3},{8,12},{9,5},{1... | collective-permute-start | bytes 983048 | tf_op jit(solution)/shard_map/ppermute | solution.py:29
  66.2 11.8 %collective-permute-start.23 = (f32[480,128]{1,0:T(8,128)S(1)}, f32[480,128]{1,0:T(8,128)S(1)}, u32[]{:S(2)}, u32[]{:S(2)}) collective-permute-start(f32[480,128]{1,0:T(8,128)S(1)} %get-tuple-element.35.own2), channel_id=1, source_target_pairs={{0,4},{1,13},{2,6},{3,15},{4,8},{5,1},{6,10},{7,3},{8,12},{9,5},{1... | collective-permute-start | bytes 737288 | tf_op jit(solution)/shard_map/ppermute | solution.py:29
  66.2 11.9 %collective-permute-start.26 = (f32[480,128]{1,0:T(8,128)S(1)}, f32[480,128]{1,0:T(8,128)S(1)}, u32[]{:S(2)}, u32[]{:S(2)}) collective-permute-start(f32[480,128]{1,0:T(8,128)S(1)} %collective-permute-done.25.near), channel_id=1, source_target_pairs={{0,4},{1,13},{2,6},{3,15},{4,8},{5,1},{6,10},{7,3},{8,12},{9,5},{1... | collective-permute-start | bytes 737288 | tf_op jit(solution)/shard_map/ppermute | solution.py:29
  67.4 11.2 %collective-permute-start.33 = (f32[640,128]{1,0:T(8,128)S(1)}, f32[640,128]{1,0:T(8,128)S(1)}, u32[]{:S(2)}, u32[]{:S(2)}) collective-permute-start(f32[640,128]{1,0:T(8,128)S(1)} %collective-permute-done.31.near), channel_id=1, source_target_pairs={{0,1},{1,0},{2,3},{3,2},{4,5},{5,4},{6,7},{7,6},{8,9},{9,8},{10,11... | collective-permute-start | bytes 983048 | tf_op jit(solution)/shard_map/ppermute | solution.py:17
  69.5 9.1 %collective-permute-start.30 = (f32[640,128]{1,0:T(8,128)S(1)}, f32[640,128]{1,0:T(8,128)S(1)}, u32[]{:S(2)}, u32[]{:S(2)}) collective-permute-start(f32[640,128]{1,0:T(8,128)S(1)} %collective-permute-done.29.near2), channel_id=1, source_target_pairs={{0,1},{1,0},{2,3},{3,2},{4,5},{5,4},{6,7},{7,6},{8,9},{9,8},{10,11... | collective-permute-start | bytes 983048 | tf_op jit(solution)/shard_map/ppermute | solution.py:17
  69.5 9.2 %collective-permute-start.34 = (f32[640,128]{1,0:T(8,128)S(1)}, f32[640,128]{1,0:T(8,128)S(1)}, u32[]{:S(2)}, u32[]{:S(2)}) collective-permute-start(f32[640,128]{1,0:T(8,128)S(1)} %collective-permute-done.32.opposite), channel_id=1, source_target_pairs={{0,1},{1,0},{2,3},{3,2},{4,5},{5,4},{6,7},{7,6},{8,9},{9,8},{10,11... | collective-permute-start | bytes 983048 | tf_op jit(solution)/shard_map/ppermute | solution.py:17
  78.0 7.8 %collective-permute-start.27 = (f32[480,128]{1,0:T(8,128)S(1)}, f32[480,128]{1,0:T(8,128)S(1)}, u32[]{:S(2)}, u32[]{:S(2)}) collective-permute-start(f32[480,128]{1,0:T(8,128)S(1)} %collective-permute-done.25.near), channel_id=1, source_target_pairs={{0,1},{1,0},{2,3},{3,2},{4,5},{5,4},{6,7},{7,6},{8,9},{9,8},{10,11... | collective-permute-start | bytes 737288 | tf_op jit(solution)/shard_map/ppermute | solution.py:17
  78.1 7.7 %collective-permute-start.24 = (f32[480,128]{1,0:T(8,128)S(1)}, f32[480,128]{1,0:T(8,128)S(1)}, u32[]{:S(2)}, u32[]{:S(2)}) collective-permute-start(f32[480,128]{1,0:T(8,128)S(1)} %collective-permute-done.23.near2), channel_id=1, source_target_pairs={{0,1},{1,0},{2,3},{3,2},{4,5},{5,4},{6,7},{7,6},{8,9},{9,8},{10,11... | collective-permute-start | bytes 737288 | tf_op jit(solution)/shard_map/ppermute | solution.py:17
  78.6 7.3 %collective-permute-start.28 = (f32[480,128]{1,0:T(8,128)S(1)}, f32[480,128]{1,0:T(8,128)S(1)}, u32[]{:S(2)}, u32[]{:S(2)}) collective-permute-start(f32[480,128]{1,0:T(8,128)S(1)} %collective-permute-done.26.opposite), channel_id=1, source_target_pairs={{0,1},{1,0},{2,3},{3,2},{4,5},{5,4},{6,7},{7,6},{8,9},{9,8},{10,11... | collective-permute-start | bytes 737288 | tf_op jit(solution)/shard_map/ppermute | solution.py:17
